TPU v7x, 32 devices: a whole 2x2x4 slice. The times are simulated.
32 devices in a mesh: docs: 8 (over y, x, core), feat: 4 (over z).
Axes of the slice: x: 2, y: 2, z: 4, core: 2. Of those that a mesh axis runs over, the one named last changes fastest.
Arguments:
- feature_ids: int32 [2048, 512], P('docs', 'feat'), may hold values from 0 to 32767
- feature_weights: bfloat16 [2048, 512], P('docs', 'feat'), may hold values from 1 to 8
- projection: bfloat16 [131072, 256], P('feat'), may hold values from -6 to 6
- bucket_lists: int32 [2048, 32, 2], P('docs', 'feat'), may hold values from 0 to 4095, as said below
- bucket_counts: int32 [256, 4], P('docs', 'feat'), may hold values from 0 to 128, as said below
Outputs:
- cosine_tiles: float32 [256, 4, 128, 128], P('docs', 'feat')
- affinity: float32 [256, 4, 128], P('docs', 'feat')
Inputs may be any that keep to these rules, and one draw needn't show every extreme that they name: bucket_lists[i, b] = (owner, slot): owner is an index of docs, slot a slot of that owner; bucket t is slots t * 128 to (t + 1) * 128 - 1. Within one band block, no two entries share owner and slot. The entries of one device (its documents times its band block) name one owner at most 512 times, and in every band block some owner is named 512 times by every device. bucket_counts[o * 32 + t, f] is the number of entries of band block f in bucket t of owner o; they fill exactly its first slots.
All inputs are finite; a program needn't handle non-finite values.
Results may differ from a plain program's by a relative error of at most 0.0007.
Values may be sent and summed in bfloat16 or wider, within the bound.
No kernel may reach another device: no remote copies, remote signals or barrier semaphores. Data moves between devices by JAX's collectives and lax.ppermute only.
A program may use at most 128 MiB of HBM per device.

v0:
```python
import jax
import jax.numpy as jnp
from jax import lax
from jax.sharding import PartitionSpec as P

TILE = 128


epsilon = 1e-06


def to_unit(signature):
    scale = lax.rsqrt(jnp.sum(signature * signature, axis=1, keepdims=True) + epsilon)
    return (signature * scale).astype(jnp.bfloat16)


def per_device(feature_ids, feature_weights, projection, bucket_lists, bucket_counts):
    doc_rows, entry_width = feature_ids.shape
    sig_width = projection.shape[1]
    block_docs = min(64, doc_rows)

    def project_block(pieces):
        gathered = projection[pieces[0]]
        return jnp.einsum("dn,dns->ds", pieces[1], gathered, preferred_element_type=jnp.float32)

    id_blocks = feature_ids.reshape(doc_rows // block_docs, block_docs, entry_width)
    weight_blocks = feature_weights.reshape(doc_rows // block_docs, block_docs, entry_width)
    partial_value = lax.map(project_block, (id_blocks, weight_blocks)).reshape(doc_rows, sig_width)
    unit_sig = to_unit(lax.psum(partial_value, "feat"))
    band_count = bucket_lists.shape[1]
    tile_count = bucket_counts.shape[0]
    room_size = tile_count * TILE
    bucket_table = jnp.zeros((room_size, sig_width), jnp.bfloat16)
    all_unit, all_lists = (
        lax.all_gather(unit_sig, "docs", axis=0, tiled=True),
        lax.all_gather(bucket_lists, "docs", axis=0, tiled=True),
    )
    my_index = lax.axis_index("docs")
    for band_step in range(band_count):
        target = jnp.where(
            all_lists[:, band_step, 0] == my_index, all_lists[:, band_step, 1], room_size
        )
        bucket_table = bucket_table.at[target].set(all_unit, mode="drop")
    tile_rows = bucket_table.reshape(tile_count, TILE, sig_width)
    products = jnp.einsum("tis,tjs->tij", tile_rows, tile_rows, preferred_element_type=jnp.float32)
    filled = bucket_counts[:, 0]
    filled_mask = (jnp.arange(TILE)[None, :] < filled[:, None]).astype(jnp.float32)
    cosine = products * filled_mask[:, :, None] * filled_mask[:, None, :]
    self_term = jnp.diagonal(cosine, axis1=1, axis2=2)
    divisor = jnp.maximum(filled - 1, 1).astype(jnp.float32)
    affinity = (jnp.sum(cosine, axis=2) - self_term) / divisor[:, None]
    return (cosine[:, None], affinity[:, None])


def solution(mesh):
    placed = (
        P("docs", "feat"),
        P("docs", "feat"),
        P("feat", None),
        P("docs", "feat", None),
        P("docs", "feat"),
    )
    return jax.shard_map(
        per_device,
        mesh=mesh,
        in_specs=placed,
        out_specs=(P("docs", "feat", None, None), P("docs", "feat", None)),
        check_vma=False,
    )
```

profile of v0, /device:TPU:0, one launch (start us, length us, event | category | flops | bytes accessed | tf_op | source)
XLA Modules:
  0.0 352.4 jit_solution(2145841767992811861)
XLA Ops:
  7.2 175.2 %while.10 = (s32[]{:T(128)}, f32[4,64,256]{2,1,0:T(8,128)}, bf16[4,64,128]{2,1,0:T(8,128)(2,1)}, s32[4,64,128]{2,1,0:T(8,128)}, bf16[32768,256]{1,0:T(8,128)(2,1)}, /*index=5*/s32[]{:T(128)}) while((s32[]{:T(128)}, f32[4,64,256]{2,1,0:T(8,128)}, bf16[4,64,128]{2,1,0:T(8,128)(2,1)}, s32[4,64,128]{2,1,0:T(8,128)}, bf16[32768,256]{1,0:T(8,128)(2,1)}, ...), condition=%wide.region_1.2_spmd, body=%wide.region_0.1_spmd.sunk | while | flops 4227074 | bytes 12927565 | solution.py:28
  7.3 0.8 fusion.25
  8.0 38.8 %gather_fusion = bf16[8192,256]{1,0:T(8,128)(2,1)} fusion(bf16[32768,256]{1,0:T(8,128)(2,1)} %get-tuple-element.103, s32[8192]{0:T(1024)S(1)} %fusion.25), kind=kCustom, calls=%fused_computation.clone.1 | custom fusion | bytes 8421376 | tf_op jit(solution)/shard_map/while/body/eval_jaxpr/gather | solution.py:23
  46.8 0.7 dynamic-slice_bitcast_fusion.2
  47.6 2.8 fusion.26
  51.0 0.8 fusion.25
  51.8 38.8 %gather_fusion = bf16[8192,256]{1,0:T(8,128)(2,1)} fusion(bf16[32768,256]{1,0:T(8,128)(2,1)} %get-tuple-element.103, s32[8192]{0:T(1024)S(1)} %fusion.25), kind=kCustom, calls=%fused_computation.clone.1 | custom fusion | bytes 8421376 | tf_op jit(solution)/shard_map/while/body/eval_jaxpr/gather | solution.py:23
  90.6 0.7 dynamic-slice_bitcast_fusion.2
  91.4 2.8 fusion.26
  94.8 0.8 fusion.25
  95.6 38.8 %gather_fusion = bf16[8192,256]{1,0:T(8,128)(2,1)} fusion(bf16[32768,256]{1,0:T(8,128)(2,1)} %get-tuple-element.103, s32[8192]{0:T(1024)S(1)} %fusion.25), kind=kCustom, calls=%fused_computation.clone.1 | custom fusion | bytes 8421376 | tf_op jit(solution)/shard_map/while/body/eval_jaxpr/gather | solution.py:23
  135.1 2.8 fusion.26
  138.6 0.8 fusion.25
  139.4 38.8 %gather_fusion = bf16[8192,256]{1,0:T(8,128)(2,1)} fusion(bf16[32768,256]{1,0:T(8,128)(2,1)} %get-tuple-element.103, s32[8192]{0:T(1024)S(1)} %fusion.25), kind=kCustom, calls=%fused_computation.clone.1 | custom fusion | bytes 8421376 | tf_op jit(solution)/shard_map/while/body/eval_jaxpr/gather | solution.py:23
  178.9 2.8 fusion.26
  182.5 38.1 %all-reduce.2.cloned.1.call-done = f32[256,256]{1,0:T(8,128)} async-done(((f32[256,256]{1,0:T(8,128)}), f32[256,256]{1,0:T(8,128)}) %all-reduce.2.cloned.1.call-update) | async-done | bytes 262160 | tf_op jit(solution)/shard_map/psum | solution.py:29
  220.6 1.1 multiply_reduce_fusion
  221.7 1.7 multiply_convert_fusion
  223.4 9.0 %all_gather.6 = s32[2048,8,2]{0,2,1:T(2,128)S(1)} all-gather(s32[256,8,2]{0,2,1:T(2,128)S(1)} %copy-done.2), channel_id=1, replica_groups=mesh['docs'=8,'feat'=4] {'docs'}, dimensions={0}, use_global_device_ids=true | all-gather | bytes 147456 | tf_op jit(solution)/shard_map/all_gather | solution.py:36
  232.7 14.1 %all-gather.2.cloned.1.call-done = bf16[2048,256]{1,0:T(8,128)(2,1)} async-done(((bf16[256,256]{1,0:T(8,128)(2,1)}), bf16[2048,256]{1,0:T(8,128)(2,1)}) %all-gather.2.cloned.1.call-update) | async-done | bytes 1048592 | tf_op jit(solution)/shard_map/all_gather | solution.py:35
  246.8 10.4 %scatter_custom_fusion = bf16[4096,256]{1,0:T(8,128)(2,1)S(1)} fusion(s32[2048]{0:T(1024)S(1)} %bitcast.97, bf16[2048,256]{1,0:T(8,128)(2,1)} %all-gather.2.cloned.1.call-done, bf16[]{:T(256)} %constant.12.clone.1), kind=kCustom, calls=%fused_computation.18 | custom fusion | bytes 2097664 | tf_op jit(solution)/shard_map/scatter | solution.py:43
  257.2 10.4 %scatter_fusion = bf16[4096,256]{1,0:T(8,128)(2,1)S(1)} fusion(bf16[4096,256]{1,0:T(8,128)(2,1)S(1)} %scatter_custom_fusion, s32[2048]{0:T(1024)S(1)} %bitcast.96, bf16[2048,256]{1,0:T(8,128)(2,1)S(1)} %copy-done), kind=kCustom, calls=%fused_computation.3 | custom fusion | bytes 3153920 | tf_op jit(solution)/shard_map/scatter | solution.py:43
  267.6 10.6 %scatter_fusion.1 = bf16[4096,256]{1,0:T(8,128)(2,1)S(1)} fusion(bf16[4096,256]{1,0:T(8,128)(2,1)S(1)} %scatter_fusion, s32[2048]{0:T(1024)S(1)} %bitcast.95, bf16[2048,256]{1,0:T(8,128)(2,1)S(1)} %copy-done), kind=kCustom, calls=%fused_computation.4 | custom fusion | bytes 3153920 | tf_op jit(solution)/shard_map/scatter | solution.py:43
  278.2 10.4 %scatter_fusion.2 = bf16[4096,256]{1,0:T(8,128)(2,1)S(1)} fusion(bf16[4096,256]{1,0:T(8,128)(2,1)S(1)} %scatter_fusion.1, s32[2048]{0:T(1024)S(1)} %bitcast.94, bf16[2048,256]{1,0:T(8,128)(2,1)S(1)} %copy-done), kind=kCustom, calls=%fused_computation.5 | custom fusion | bytes 3153920 | tf_op jit(solution)/shard_map/scatter | solution.py:43
  288.6 10.4 %scatter_fusion.3 = bf16[4096,256]{1,0:T(8,128)(2,1)S(1)} fusion(bf16[4096,256]{1,0:T(8,128)(2,1)S(1)} %scatter_fusion.2, s32[2048]{0:T(1024)S(1)} %bitcast.93, bf16[2048,256]{1,0:T(8,128)(2,1)S(1)} %copy-done), kind=kCustom, calls=%fused_computation.6 | custom fusion | bytes 3153920 | tf_op jit(solution)/shard_map/scatter | solution.py:43
  299.0 10.6 %scatter_fusion.4 = bf16[4096,256]{1,0:T(8,128)(2,1)S(1)} fusion(bf16[4096,256]{1,0:T(8,128)(2,1)S(1)} %scatter_fusion.3, s32[2048]{0:T(1024)S(1)} %bitcast.92, bf16[2048,256]{1,0:T(8,128)(2,1)S(1)} %copy-done), kind=kCustom, calls=%fused_computation.7 | custom fusion | bytes 3153920 | tf_op jit(solution)/shard_map/scatter | solution.py:43
  309.6 10.4 %scatter_fusion.5 = bf16[4096,256]{1,0:T(8,128)(2,1)S(1)} fusion(bf16[4096,256]{1,0:T(8,128)(2,1)S(1)} %scatter_fusion.4, s32[2048]{0:T(1024)S(1)} %bitcast.91, bf16[2048,256]{1,0:T(8,128)(2,1)S(1)} %copy-done), kind=kCustom, calls=%fused_computation.8 | custom fusion | bytes 3153920 | tf_op jit(solution)/shard_map/scatter | solution.py:43
  320.0 10.7 %scatter_fusion.6 = bf16[4096,256]{1,0:T(8,128)(2,1)S(1)} fusion(bf16[4096,256]{1,0:T(8,128)(2,1)S(1)} %scatter_fusion.5, s32[2048]{0:T(1024)S(1)} %bitcast.90, bf16[2048,256]{1,0:T(8,128)(2,1)S(1)} %copy-done), kind=kCustom, calls=%fused_computation.9 | custom fusion | bytes 3153920 | tf_op jit(solution)/shard_map/scatter | solution.py:43
  330.7 1.9 fusion.15
  332.6 8.6 %copy.13 = f32[32,128,128]{0,2,1:T(8,128)} copy(f32[32,128,128]{1,2,0:T(8,128)} %get-tuple-element.55) | data formatting | bytes 4194304 | tf_op jit(solution)/shard_map/mul | solution.py:48
  341.2 1.8 gather_fusion.1
  343.7 1.8 copy.15
  (27 shorter events, 5.2 us)
Async XLA Ops:
  7.2 213.4 %all-reduce.2.cloned.1.call-start = ((), (), s32[]{:S(2)}) async-start(), calls=%async_computation | async-start | bytes 524288 | tf_op jit(solution)/shard_map/psum | solution.py:29
  7.2 216.2 %copy-start.2 = (s32[256,8,2]{0,2,1:T(2,128)S(1)}, s32[256,8,2]{0,2,1:T(2,128)}, u32[]{:S(2)}) copy-start(s32[256,8,2]{0,2,1:T(2,128)} %param.10) | copy-start | bytes 49156
  7.2 225.2 %copy-start.3 = (s32[32,1]{0,1:T(1,128)S(1)}, s32[32,1]{0,1:T(1,128)}, u32[]{:S(2)}) copy-start(s32[32,1]{0,1:T(1,128)} %param.11) | copy-start | bytes 388
  182.4 64.4 %all-gather.2.cloned.1.call-start = ((), (), s32[]{:S(2)}) async-start(), calls=%async_computation.1 | async-start | bytes 1179648 | tf_op jit(solution)/shard_map/all_gather | solution.py:35
  246.8 10.4 %copy-start = (bf16[2048,256]{1,0:T(8,128)(2,1)S(1)}, bf16[2048,256]{1,0:T(8,128)(2,1)}, u32[]{:S(2)}) copy-start(bf16[2048,256]{1,0:T(8,128)(2,1)} %all-gather.2.cloned.1.call-done) | copy-start | bytes 3145732
  332.6 11.2 %copy-start.1 = (f32[32,128,128]{1,2,0:T(8,128)S(1)}, f32[32,128,128]{1,2,0:T(8,128)}, u32[]{:S(2)}) copy-start(f32[32,128,128]{1,2,0:T(8,128)} %get-tuple-element.55) | copy-start | bytes 6291460
Sparse Core Ops, SparseCore 0:
  182.5 37.9 all-reduce.1
  223.5 23.2 all-gather.1
where the time goes:
time: 353 us; the launch traced here: 352 us
  local copies, waits for them, and re-layouts  257 us (73%)
  waiting for transfers between devices  52.3 us (15%)
  between operations  14.2 us (4%)
  matrix products  13.2 us (4%)
  blocking collectives  9.03 us (3%)
  other arithmetic  6.07 us (2%)
    gather x4, local copies, waits for them, and re-layouts, project_block(): gathered = projection[pieces[0]]  155 us
    scatter x8, local copies, waits for them, and re-layouts, per_device(): bucket_table = bucket_table.at[target].set(all_unit, mode='drop')  83.8 us
    psum x1, waiting for transfers between devices, per_device(): unit_sig = to_unit(lax.psum(partial_value, 'feat'))  38.1 us
    all_gather x1, waiting for transfers between devices, per_device(): lax.all_gather(unit_sig, 'docs', axis=0, tiled=True)  14.1 us
    dot_general x4, matrix products, project_block(): jnp.einsum('dn,dns->ds', pieces[1], gathered, preferred_element_type=jnp....  11.3 us
    all_gather x1, blocking collectives, per_device(): lax.all_gather(bucket_lists, 'docs', axis=0, tiled=True)  9.03 us
    mul x1, local copies, waits for them, and re-layouts, per_device(): cosine = products * filled_mask[:, :, None] * filled_mask[:, None, :]  8.58 us
  transfers between devices with their start and end apart: 2, of which 2 were waited for; matrix products, arithmetic and copies ran while one was open for 0% of the time, Pallas kernels for 0%

commit v1 on v0

v1 whole, which is shorter than its diff:
```python
import functools

import jax
import jax.numpy as jnp
from jax import lax
from jax.experimental import pallas as pl
from jax.experimental.pallas import tpu as pltpu
from jax.sharding import PartitionSpec as P

TILE = 128
LO = 128
EPSILON = 1e-06


def _fits(count, most):
    while count % most:
        most -= 1
    return most


def _signature_kernel(
    docs, entries, hi_n, stride, unroll, k_step, parts,
    ids_ref, w_ref, proj_ref, *rest,
):
    out_refs = rest[:parts]
    proj, counts, lhs, weights, total, sems = rest[parts:]
    chunks, chunk_rows, _ = proj.shape

    def chunk_copy(c):
        return pltpu.make_async_copy(
            proj_ref.at[pl.ds(c * chunk_rows, chunk_rows), :], proj.at[c], sems.at[c]
        )

    for c in range(chunks):
        chunk_copy(c).start()
    weights[...] = w_ref[...].astype(jnp.float32)

    def pair(p):
        iota_hi = lax.broadcasted_iota(jnp.int32, (hi_n, entries), 0).astype(jnp.bfloat16)
        iota_lo = lax.broadcasted_iota(jnp.int32, (LO, entries), 0).astype(jnp.bfloat16)
        one_hi = jnp.ones((hi_n, entries), jnp.bfloat16)
        zero_hi = jnp.zeros((hi_n, entries), jnp.bfloat16)
        zero_lo = jnp.zeros((LO, entries), jnp.bfloat16)
        his, los = [], []
        for e in range(2):
            ids = ids_ref[pl.ds(2 * p + e, 1), :]
            w = weights[pl.ds(2 * p + e, 1), :].astype(jnp.bfloat16)
            hi = (ids // LO).astype(jnp.float32).astype(jnp.bfloat16)
            lo = (ids % LO).astype(jnp.float32).astype(jnp.bfloat16)
            his.append(jnp.where(iota_hi == hi, one_hi, zero_hi))
            lo_w = jnp.where(iota_lo == lo, jnp.broadcast_to(w, (LO, entries)), zero_lo)
            los.append(jnp.concatenate([lo_w, zero_lo] if e == 0 else [zero_lo, lo_w], axis=1))
        r = lax.dot_general(
            jnp.concatenate(his, axis=1), jnp.concatenate(los, axis=0),
            (((1,), (1,)), ((), ())), preferred_element_type=jnp.float32,
        )
        for e in range(2):
            for t in range(hi_n // 8):
                counts[pl.ds(t * 8 * stride + 2 * p + e, 8, stride=stride), :] = r[
                    t * 8:(t + 1) * 8, e * LO:(e + 1) * LO
                ]

    def pairs(i, _):
        for u in range(unroll):
            pair(i * unroll + u)
        return 0

    lax.fori_loop(0, docs // 2 // unroll, pairs, 0)

    per_chunk = chunk_rows // LO
    for c in range(chunks):
        chunk_copy(c).wait()

        def multiply(k, _, c=c):
            for q in range(k_step):
                row = pl.multiple_of((c * per_chunk + k_step * k + q) * stride, 8)
                a = counts[pl.ds(row, docs), :]
                top = a.astype(jnp.bfloat16)
                lhs[:docs, q * LO:(q + 1) * LO] = top
                lhs[docs:, q * LO:(q + 1) * LO] = (a - top.astype(jnp.float32)).astype(jnp.bfloat16)
            first = pl.multiple_of(k * k_step * LO, k_step * LO)
            r = jnp.dot(
                lhs[...], proj[c, pl.ds(first, k_step * LO), :],
                preferred_element_type=jnp.float32,
            )
            r = r[:docs] + r[docs:]
            if c == 0:
                total[...] = jnp.where(k == 0, r, total[...] + r)
            else:
                total[...] += r
            return 0

        lax.fori_loop(0, per_chunk // k_step, multiply, 0)

    part_rows = docs // parts
    me = lax.axis_index("feat")
    for k in range(parts):
        row = pl.multiple_of((me ^ k) * part_rows, part_rows)
        out_refs[k][...] = total[pl.ds(row, part_rows), :]


def _signature_parts(ids, w, projection, parts):
    docs, entries = ids.shape
    feats, width = projection.shape
    hi_n = feats // LO
    chunks = 4
    stride = docs + 8
    k_step = _fits(hi_n // chunks, 32)
    unroll = _fits(docs // 2, 16)
    return pl.pallas_call(
        functools.partial(
            _signature_kernel, docs, entries, hi_n, stride, unroll, k_step, parts
        ),
        out_shape=[jax.ShapeDtypeStruct((docs // parts, width), jnp.float32)] * parts,
        in_specs=[
            pl.BlockSpec(memory_space=pltpu.VMEM),
            pl.BlockSpec(memory_space=pltpu.VMEM),
            pl.BlockSpec(memory_space=pl.ANY),
        ],
        out_specs=[pl.BlockSpec(memory_space=pltpu.VMEM)] * parts,
        scratch_shapes=[
            pltpu.VMEM((chunks, feats // chunks, width), jnp.bfloat16),
            pltpu.VMEM((hi_n * stride, LO), jnp.float32),
            pltpu.VMEM((2 * docs, k_step * LO), jnp.bfloat16),
            pltpu.VMEM((docs, entries), jnp.float32),
            pltpu.VMEM((docs, width), jnp.float32),
            pltpu.SemaphoreType.DMA((chunks,)),
        ],
        compiler_params=pltpu.CompilerParams(vmem_limit_bytes=60 << 20),
    )(ids, w, projection)


def _unit_kernel(*refs):
    total = refs[0][...]
    for ref in refs[1:-1]:
        total = total + ref[...]
    scale = lax.rsqrt(jnp.sum(total * total, axis=1, keepdims=True) + EPSILON)
    refs[-1][...] = (total * scale).astype(jnp.bfloat16)


def _unit(parts):
    return pl.pallas_call(
        _unit_kernel,
        out_shape=jax.ShapeDtypeStruct(parts[0].shape, jnp.bfloat16),
        in_specs=[pl.BlockSpec(memory_space=pltpu.VMEM)] * len(parts),
        out_specs=pl.BlockSpec(memory_space=pltpu.VMEM),
    )(*parts)


def _source_kernel(docs, tiles, rows_dev, shard, targets_ref, out_ref):
    me_docs = lax.axis_index("docs")
    me_feat = lax.axis_index("feat")
    sub = docs // 128
    base = me_docs * (tiles * TILE)
    iota_lo = lax.broadcasted_iota(jnp.int32, (TILE, 128), 0).astype(jnp.bfloat16)
    iota_hi = lax.broadcasted_iota(jnp.int32, (tiles, 128), 0).astype(jnp.bfloat16)
    one_lo = jnp.ones((TILE, 128), jnp.bfloat16)
    zero_lo = jnp.zeros((TILE, 128), jnp.bfloat16)
    zero_hi = jnp.zeros((tiles, 128), jnp.bfloat16)
    lane = lax.broadcasted_iota(jnp.int32, (1, 128), 1)
    out_ref[...] = jnp.zeros_like(out_ref)

    def step(i, _):
        block = targets_ref[pl.ds(pl.multiple_of(i * 8, 8), 8), :] - base
        dev = ((i * 8) // rows_dev) ^ me_docs
        dev_row = jnp.full((tiles, 128), dev.astype(jnp.float32), jnp.float32).astype(jnp.bfloat16)
        los, his = [], []
        for r in range(8):
            row = block[r:r + 1, :]
            hi = (row >> 7).astype(jnp.float32).astype(jnp.bfloat16)
            lo = (row & 127).astype(jnp.float32).astype(jnp.bfloat16)
            place = ((r % sub) * 128 + lane) ^ (me_feat * shard)
            place = place.astype(jnp.float32).astype(jnp.bfloat16)
            los.append(jnp.where(iota_lo == lo, one_lo, zero_lo))
            here = iota_hi == hi
            his.append(jnp.concatenate([
                jnp.where(here, jnp.broadcast_to(place, (tiles, 128)), zero_hi),
                jnp.where(here, dev_row, zero_hi),
            ], axis=0))
        out_ref[...] += lax.dot_general(
            jnp.concatenate(los, axis=1), jnp.concatenate(his, axis=1),
            (((1,), (1,)), ((), ())), preferred_element_type=jnp.float32,
        )
        return 0

    lax.fori_loop(0, targets_ref.shape[0] // 8, step, 0)


def _sources(targets, docs, tiles, rows_dev, shard):
    return pl.pallas_call(
        functools.partial(_source_kernel, docs, tiles, rows_dev, shard),
        out_shape=jax.ShapeDtypeStruct((TILE, 2 * tiles), jnp.float32),
        in_specs=[pl.BlockSpec(memory_space=pltpu.VMEM)],
        out_specs=pl.BlockSpec(memory_space=pltpu.VMEM),
    )(targets)


def _tiles_kernel(blocks, group, counts_ref, source_ref, *rest):
    unit_refs = rest[:blocks]
    cosine_hbm, affinity_ref, cosine, sems = rest[blocks:]
    tiles = cosine.shape[0]
    docs = unit_refs[0].shape[0]
    lane = lax.broadcasted_iota(jnp.int32, (TILE, docs), 1).astype(jnp.bfloat16)
    one = jnp.ones((TILE, docs), jnp.bfloat16)
    zero = jnp.zeros((TILE, docs), jnp.bfloat16)
    row_of = lax.broadcasted_iota(jnp.int32, (TILE, TILE), 0)
    col_of = lax.broadcasted_iota(jnp.int32, (TILE, TILE), 1)
    place = source_ref[:, :tiles] + source_ref[:, tiles:] * docs

    def copy_out(g):
        span = pl.ds(g * group, group)
        return pltpu.make_async_copy(cosine.at[span], cosine_hbm.at[span], sems.at[g])

    for g in range(tiles // group):
        total = jnp.zeros((group * TILE, unit_refs[0].shape[1]), jnp.float32)
        sources = [
            jnp.broadcast_to(place[:, t:t + 1], (TILE, docs))
            for t in range(g * group, (g + 1) * group)
        ]
        for b in range(blocks):
            pick = jnp.concatenate([
                jnp.where(lane == (s - b * docs).astype(jnp.bfloat16), one, zero) for s in sources
            ], axis=0)
            total = total + jnp.dot(pick, unit_refs[b][...], preferred_element_type=jnp.float32)
        table = total.astype(jnp.bfloat16)
        for j in range(group):
            t = g * group + j
            rows = table[j * TILE:(j + 1) * TILE]
            filled = counts_ref[t, 0]
            products = lax.dot_general(
                rows, rows, (((1,), (1,)), ((), ())), preferred_element_type=jnp.float32
            )
            products = jnp.where(jnp.maximum(row_of, col_of) < filled, products, 0.0)
            cosine[t] = products
            others = jnp.sum(jnp.where(row_of == col_of, 0.0, products), axis=0, keepdims=True)
            divisor = jnp.full((1, TILE), jnp.maximum(filled - 1, 1).astype(jnp.float32))
            affinity_ref[t:t + 1, :] = others / divisor
        copy_out(g).start()
    for g in range(tiles // group):
        copy_out(g).wait()


def _tiles(counts, source, units):
    tiles = counts.shape[0]
    group = _fits(tiles, 4)
    return pl.pallas_call(
        functools.partial(_tiles_kernel, len(units), group),
        out_shape=[
            jax.ShapeDtypeStruct((tiles, TILE, TILE), jnp.float32),
            jax.ShapeDtypeStruct((tiles, TILE), jnp.float32),
        ],
        in_specs=[pl.BlockSpec(memory_space=pltpu.SMEM)]
        + [pl.BlockSpec(memory_space=pltpu.VMEM)] * (1 + len(units)),
        out_specs=[pl.BlockSpec(memory_space=pl.ANY), pl.BlockSpec(memory_space=pltpu.VMEM)],
        scratch_shapes=[
            pltpu.VMEM((tiles, TILE, TILE), jnp.float32),
            pltpu.SemaphoreType.DMA((tiles // group,)),
        ],
        compiler_params=pltpu.CompilerParams(vmem_limit_bytes=48 << 20),
    )(counts, source, *units)


def solution(mesh):
    n_docs, n_feat = mesh.shape["docs"], mesh.shape["feat"]

    def send(x, axis, size, k):
        return lax.ppermute(x, axis, [(i, i ^ k) for i in range(size)])

    def per_device(ids, w, projection, lists, counts):
        docs = ids.shape[0]
        tiles = counts.shape[0]
        shard = docs // n_feat
        targets = (lists[:, :, 0] * (tiles * TILE) + lists[:, :, 1]).T.reshape(-1, 128)
        rows_dev = targets.shape[0]
        targets = lax.all_gather(targets, "docs", axis=0, tiled=True)
        parts = _signature_parts(ids, w, projection, n_feat)
        received = [send(parts[k], "feat", n_feat, k) for k in range(1, n_feat)]
        source = _sources(targets, docs, tiles, rows_dev, shard)
        own = _unit([parts[0]] + received)
        own = jnp.concatenate([own] + [send(own, "feat", n_feat, k) for k in range(1, n_feat)])
        near = [own] + [send(own, "docs", n_docs, k) for k in range(2, n_docs, 2)]
        units = []
        for block in near:
            units += [block, send(block, "docs", n_docs, 1)]
        cosine, affinity = _tiles(counts, source, units)
        return cosine[:, None], affinity[:, None]

    placed = (
        P("docs", "feat"),
        P("docs", "feat"),
        P("feat", None),
        P("docs", "feat", None),
        P("docs", "feat"),
    )
    return jax.shard_map(
        per_device,
        mesh=mesh,
        in_specs=placed,
        out_specs=(P("docs", "feat", None, None), P("docs", "feat", None)),
        check_vma=False,
    )
```

time: 353 us -> 79.7 us (0.23)
  local copies, waits for them, and re-layouts: 257 us -> 1.57 us
  waiting for transfers between devices: 52.3 us -> 13.1 us
  Pallas kernels: 0 us -> 38.9 us
  starting transfers between devices: 0.08 us -> 13.7 us
  between operations: 14.2 us -> 0.87 us
  matrix products: 13.2 us -> 0 us
  other arithmetic: 6.07 us -> 0.77 us
    gather x5 -> x0, local copies, waits for them, and re-layouts: 157 us -> none  [the longest x4 155 us: project_block(): gathered = projection[pieces[0]]]
    scatter x8 -> x0, local copies, waits for them, and re-layouts: 83.8 us -> none  [per_device(): bucket_table = bucket_table.at[target].set(all_unit, mode='drop')]
    pallas_call x0 -> x4, Pallas kernels: none -> 38.9 us  [the longest x1 19.9 us: _signature_parts(): pl.pallas_call(functools.partial(_signature_kernel, docs, entries, hi_n,...]
    psum x1 -> x0, waiting for transfers between devices: 38.1 us -> none  [per_device(): unit_sig = to_unit(lax.psum(partial_value, 'feat'))]
    all_gather x1 -> x0, waiting for transfers between devices: 14.1 us -> none  [per_device(): lax.all_gather(unit_sig, 'docs', axis=0, tiled=True)]
    ppermute x0 -> x13, starting transfers between devices: none -> 13.7 us  [send(): return lax.ppermute(x, axis, [(i, i ^ k) for i in range(size)])]
    dot_general x5 -> x0, matrix products: 13.2 us -> none  [the longest x4 11.3 us: project_block(): jnp.einsum('dn,dns->ds', pieces[1], gathered, preferred_element_type=jnp....]
    ppermute x0 -> x13, waiting for transfers between devices: none -> 13.1 us  [send(): return lax.ppermute(x, axis, [(i, i ^ k) for i in range(size)])]
  transfers between devices with their start and end apart: 2 -> 13, of which waited for: 2 -> 7; matrix products, arithmetic and copies ran while one was open for 0% -> 0% of each run, Pallas kernels for 0% -> 6%
where the time goes in v1:
time: 79.7 us; the launch traced here: 79.3 us
  Pallas kernels  38.9 us (49%)
  starting transfers between devices  13.7 us (17%)
  waiting for transfers between devices  13.1 us (16%)
  blocking collectives  10.4 us (13%)
  local copies, waits for them, and re-layouts  1.57 us (2%)
  between operations  0.87 us (1%)
    pallas_call x1, Pallas kernels, _signature_parts(): pl.pallas_call(functools.partial(_signature_kernel, docs, entries, hi_n,...  19.9 us
    ppermute x13, starting transfers between devices, send(): return lax.ppermute(x, axis, [(i, i ^ k) for i in range(size)])  13.7 us
    ppermute x13, waiting for transfers between devices, send(): return lax.ppermute(x, axis, [(i, i ^ k) for i in range(size)])  13.1 us
    pallas_call x1, Pallas kernels, _tiles(): pl.pallas_call(functools.partial(_tiles_kernel, len(units), group), out_s...  12.3 us
    all_gather x1, blocking collectives, per_device(): targets = lax.all_gather(targets, 'docs', axis=0, tiled=True)  10.4 us
    pallas_call x1, Pallas kernels, _sources(): pl.pallas_call(functools.partial(_source_kernel, docs, tiles, rows_dev, s...  5.06 us
    pallas_call x1, Pallas kernels, _unit(): pl.pallas_call(_unit_kernel, out_shape=jax.ShapeDtypeStruct(parts[0].shap...  1.64 us
  transfers between devices with their start and end apart: 13, of which 7 were waited for; matrix products, arithmetic and copies ran while one was open for 0% of the time, Pallas kernels for 6%

profile of v1, /device:TPU:0, one launch (start us, length us, event | category | flops | bytes accessed | tf_op | source)
XLA Modules:
  0.0 79.3 jit_solution(8823802957800009504)
XLA Ops:
  0.7 19.9 %shard_map.69 = (f32[64,256]{1,0:T(8,128)}, f32[64,256]{1,0:T(8,128)}, f32[64,256]{1,0:T(8,128)}, f32[64,256]{1,0:T(8,128)}) custom-call(s32[256,128]{1,0:T(8,128)} %ids_ref.1, bf16[256,128]{1,0:T(8,128)(2,1)} %w_ref.1, bf16[32768,256]{1,0:T(8,128)(2,1)} %proj_ref.1), custom_call_target="tpu_custom_call" | custom-call | tf_op jit(solution)/shard_map/pallas_call | solution.py:110
  20.6 3.1 %collective-permute-start = (f32[64,256]{1,0:T(8,128)}, f32[64,256]{1,0:T(8,128)S(1)}, u32[]{:S(2)}, u32[]{:S(2)}) collective-permute-start(f32[64,256]{1,0:T(8,128)} %get-tuple-element.9), channel_id=1, source_target_pairs={{0,1},{1,0},{2,3},{3,2},{4,5},{5,4},{6,7},{7,6},{8,9},{9,8},{10,11... | collective-permute-start | bytes 196616 | tf_op jit(solution)/shard_map/ppermute | solution.py:267
  23.7 2.6 %collective-permute-start.1 = (f32[64,256]{1,0:T(8,128)}, f32[64,256]{1,0:T(8,128)S(1)}, u32[]{:S(2)}, u32[]{:S(2)}) collective-permute-start(f32[64,256]{1,0:T(8,128)} %get-tuple-element.10), channel_id=1, source_target_pairs={{0,2},{1,3},{2,0},{3,1},{4,6},{5,7},{6,4},{7,5},{8,10},{9,11},{10,... | collective-permute-start | bytes 196616 | tf_op jit(solution)/shard_map/ppermute | solution.py:267
  26.3 0.0 collective-permute-start.2
  26.3 0.0 collective-permute-done.refs_1_
  26.3 4.9 %collective-permute-done.1.refs_2_ = f32[64,256]{1,0:T(8,128)S(1)} collective-permute-done((f32[64,256]{1,0:T(8,128)}, f32[64,256]{1,0:T(8,128)S(1)}, u32[]{:S(2)}, u32[]{:S(2)}) %collective-permute-start.1) | collective-permute-done | bytes 65568 | tf_op jit(solution)/shard_map/ppermute | solution.py:267
  31.2 1.4 %collective-permute-done.2.refs_3_ = f32[64,256]{1,0:T(8,128)S(1)} collective-permute-done((f32[64,256]{1,0:T(8,128)}, f32[64,256]{1,0:T(8,128)S(1)}, u32[]{:S(2)}, u32[]{:S(2)}) %collective-permute-start.2) | collective-permute-done | bytes 65568 | tf_op jit(solution)/shard_map/ppermute | solution.py:267
  32.6 0.6 copy-done.3
  33.2 1.6 %shard_map.70 = bf16[64,256]{1,0:T(8,128)(2,1)} custom-call(f32[64,256]{1,0:T(8,128)} %get-tuple-element.8.refs_0_, f32[64,256]{1,0:T(8,128)} %copy-done.1, f32[64,256]{1,0:T(8,128)} %copy-done.2, f32[64,256]{1,0:T(8,128)} %copy-done.3), custom_call_target="tpu_custom_call" | custom-call | tf_op jit(solution)/shard_map/pallas_call | solution.py:142
  34.8 1.8 %collective-permute-start.5 = (bf16[64,256]{1,0:T(8,128)(2,1)}, bf16[64,256]{1,0:T(8,128)(2,1)S(1)}, u32[]{:S(2)}, u32[]{:S(2)}) collective-permute-start(bf16[64,256]{1,0:T(8,128)(2,1)} %shard_map.70), channel_id=1, source_target_pairs={{0,3},{1,2},{2,1},{3,0},{4,7},{5,6},{6,5},{7,4},{8,11},{9,10},{10,... | collective-permute-start | bytes 98312 | tf_op jit(solution)/shard_map/ppermute | solution.py:267
  36.6 0.0 collective-permute-start.4
  36.6 2.6 %collective-permute-start.3 = (bf16[64,256]{1,0:T(8,128)(2,1)}, bf16[64,256]{1,0:T(8,128)(2,1)S(1)}, u32[]{:S(2)}, u32[]{:S(2)}) collective-permute-start(bf16[64,256]{1,0:T(8,128)(2,1)} %shard_map.70), channel_id=1, source_target_pairs={{0,1},{1,0},{2,3},{3,2},{4,5},{5,4},{6,7},{7,6},{8,9},{9,8},{10,11... | collective-permute-start | bytes 98312 | tf_op jit(solution)/shard_map/ppermute | solution.py:267
  39.2 0.1 copy.12.counts_ref
  39.3 1.4 %collective-permute-done.5 = bf16[64,256]{1,0:T(8,128)(2,1)S(1)} collective-permute-done((bf16[64,256]{1,0:T(8,128)(2,1)}, bf16[64,256]{1,0:T(8,128)(2,1)S(1)}, u32[]{:S(2)}, u32[]{:S(2)}) %collective-permute-start.5) | collective-permute-done | bytes 32800 | tf_op jit(solution)/shard_map/ppermute | solution.py:267
  40.7 1.0 %collective-permute-done.4 = bf16[64,256]{1,0:T(8,128)(2,1)S(1)} collective-permute-done((bf16[64,256]{1,0:T(8,128)(2,1)}, bf16[64,256]{1,0:T(8,128)(2,1)S(1)}, u32[]{:S(2)}, u32[]{:S(2)}) %collective-permute-start.4) | collective-permute-done | bytes 32800 | tf_op jit(solution)/shard_map/ppermute | solution.py:267
  41.8 0.0 collective-permute-done.3
  41.8 0.8 pad_maximum_fusion.rest_0_
  42.5 2.5 %collective-permute-start.11 = (bf16[256,256]{1,0:T(8,128)(2,1)S(1)}, bf16[256,256]{1,0:T(8,128)(2,1)S(1)}, u32[]{:S(2)}, u32[]{:S(2)}) collective-permute-start(bf16[256,256]{1,0:T(8,128)(2,1)S(1)} %pad_maximum_fusion.rest_0_), channel_id=1, source_target_pairs={{0,24},{4,28},{8,16},{12,20},{16,8},{20,12},{24,0},{28,4},{1,25},{... | collective-permute-start | bytes 393224 | tf_op jit(solution)/shard_map/ppermute | solution.py:267
  45.0 0.5 collective-permute-start.9
  45.5 0.6 collective-permute-start.7
  46.1 0.1 collective-permute-start.6
  46.2 2.3 %collective-permute-done.11.rest_6_ = bf16[256,256]{1,0:T(8,128)(2,1)S(1)} collective-permute-done((bf16[256,256]{1,0:T(8,128)(2,1)S(1)}, bf16[256,256]{1,0:T(8,128)(2,1)S(1)}, u32[]{:S(2)}, u32[]{:S(2)}) %collective-permute-start.11) | collective-permute-done | bytes 131104 | tf_op jit(solution)/shard_map/ppermute | solution.py:267
  48.5 0.0 collective-permute-start.12
  48.5 1.5 %collective-permute-done.9.rest_4_ = bf16[256,256]{1,0:T(8,128)(2,1)S(1)} collective-permute-done((bf16[256,256]{1,0:T(8,128)(2,1)S(1)}, bf16[256,256]{1,0:T(8,128)(2,1)S(1)}, u32[]{:S(2)}, u32[]{:S(2)}) %collective-permute-start.9) | collective-permute-done | bytes 131104 | tf_op jit(solution)/shard_map/ppermute | solution.py:267
  50.0 0.5 collective-permute-done.7.rest_2_
  50.5 0.0 collective-permute-start.8
  50.5 10.4 %all_gather.3.targets_ref = s32[128,128]{1,0:T(8,128)} all-gather(s32[16,128]{1,0:T(8,128)S(1)} %reshape.10), channel_id=1, replica_groups=mesh['docs'=8,'feat'=4] {'docs'}, dimensions={0}, use_global_device_ids=true | all-gather | bytes 73728 | tf_op jit(solution)/shard_map/all_gather | solution.py:275
  60.9 5.1 %shard_map.68.source_ref = f32[128,64]{1,0:T(8,128)} custom-call(s32[128,128]{1,0:T(8,128)} %all_gather.3.targets_ref), custom_call_target="tpu_custom_call" | custom-call | tf_op jit(solution)/shard_map/pallas_call | solution.py:190
  66.0 0.0 collective-permute-done.8.rest_3_
  66.0 0.0 copy-start
  66.0 0.8 %copy-done = f32[128,64]{1,0:T(8,128)S(1)} copy-done((f32[128,64]{1,0:T(8,128)S(1)}, f32[128,64]{1,0:T(8,128)}, u32[]{:S(2)}) %copy-start) | copy-done | bytes 32792
  66.8 12.3 %shard_map.71 = (f32[32,128,128]{2,1,0:T(8,128)}, f32[32,128]{1,0:T(8,128)}) custom-call(s32[32,1]{1,0:T(8,128)S(1)} %copy.12.counts_ref, f32[128,64]{1,0:T(8,128)S(1)} %copy-done, bf16[256,256]{1,0:T(8,128)(2,1)S(1)} %pad_maximum_fusion.rest_0_, bf16[256,256]{1,0:T(8,128)(2,1)S(1)} %collective-permute-done.6.rest_1_, ...), custom_call_target="tpu_custom_call" | custom-call | tf_op jit(solution)/shard_map/pallas_call | solution.py:246
  (16 shorter events, 0.1 us)
Async XLA Ops:
  0.6 38.6 %copy-start.5 = (s32[32,1]{0,1:T(1,128)S(1)}, s32[32,1]{0,1:T(1,128)}, u32[]{:S(2)}) copy-start(s32[32,1]{0,1:T(1,128)} %param.9) | copy-start | bytes 388
  0.6 45.5 %copy-start.4 = (s32[256,8,2]{0,2,1:T(2,128)S(1)}, s32[256,8,2]{0,2,1:T(2,128)}, u32[]{:S(2)}) copy-start(s32[256,8,2]{0,2,1:T(2,128)} %param.8) | copy-start | bytes 49156
  20.6 5.7 %collective-permute-start = (f32[64,256]{1,0:T(8,128)}, f32[64,256]{1,0:T(8,128)S(1)}, u32[]{:S(2)}, u32[]{:S(2)}) collective-permute-start(f32[64,256]{1,0:T(8,128)} %get-tuple-element.9), channel_id=1, source_target_pairs={{0,1},{1,0},{2,3},{3,2},{4,5},{5,4},{6,7},{7,6},{8,9},{9,8},{10,11... | collective-permute-start | bytes 196616 | tf_op jit(solution)/shard_map/ppermute | solution.py:267
  23.7 7.5 %collective-permute-start.1 = (f32[64,256]{1,0:T(8,128)}, f32[64,256]{1,0:T(8,128)S(1)}, u32[]{:S(2)}, u32[]{:S(2)}) collective-permute-start(f32[64,256]{1,0:T(8,128)} %get-tuple-element.10), channel_id=1, source_target_pairs={{0,2},{1,3},{2,0},{3,1},{4,6},{5,7},{6,4},{7,5},{8,10},{9,11},{10,... | collective-permute-start | bytes 196616 | tf_op jit(solution)/shard_map/ppermute | solution.py:267
  26.3 6.3 %collective-permute-start.2 = (f32[64,256]{1,0:T(8,128)}, f32[64,256]{1,0:T(8,128)S(1)}, u32[]{:S(2)}, u32[]{:S(2)}) collective-permute-start(f32[64,256]{1,0:T(8,128)} %get-tuple-element.11), channel_id=1, source_target_pairs={{0,3},{1,2},{2,1},{3,0},{4,7},{5,6},{6,5},{7,4},{8,11},{9,10},{10,... | collective-permute-start | bytes 196616 | tf_op jit(solution)/shard_map/ppermute | solution.py:267
  26.3 6.3 %copy-start.1 = (f32[64,256]{1,0:T(8,128)}, f32[64,256]{1,0:T(8,128)S(1)}, u32[]{:S(2)}) copy-start(f32[64,256]{1,0:T(8,128)S(1)} %collective-permute-done.refs_1_) | copy-start | bytes 196612
  31.2 1.4 %copy-start.2 = (f32[64,256]{1,0:T(8,128)}, f32[64,256]{1,0:T(8,128)S(1)}, u32[]{:S(2)}) copy-start(f32[64,256]{1,0:T(8,128)S(1)} %collective-permute-done.1.refs_2_) | copy-start | bytes 196612
  32.6 0.6 copy-start.3
  34.8 5.9 %collective-permute-start.5 = (bf16[64,256]{1,0:T(8,128)(2,1)}, bf16[64,256]{1,0:T(8,128)(2,1)S(1)}, u32[]{:S(2)}, u32[]{:S(2)}) collective-permute-start(bf16[64,256]{1,0:T(8,128)(2,1)} %shard_map.70), channel_id=1, source_target_pairs={{0,3},{1,2},{2,1},{3,0},{4,7},{5,6},{6,5},{7,4},{8,11},{9,10},{10,... | collective-permute-start | bytes 98312 | tf_op jit(solution)/shard_map/ppermute | solution.py:267
  36.6 5.2 %collective-permute-start.4 = (bf16[64,256]{1,0:T(8,128)(2,1)}, bf16[64,256]{1,0:T(8,128)(2,1)S(1)}, u32[]{:S(2)}, u32[]{:S(2)}) collective-permute-start(bf16[64,256]{1,0:T(8,128)(2,1)} %shard_map.70), channel_id=1, source_target_pairs={{0,2},{1,3},{2,0},{3,1},{4,6},{5,7},{6,4},{7,5},{8,10},{9,11},{10,... | collective-permute-start | bytes 98312 | tf_op jit(solution)/shard_map/ppermute | solution.py:267
  36.6 5.2 %collective-permute-start.3 = (bf16[64,256]{1,0:T(8,128)(2,1)}, bf16[64,256]{1,0:T(8,128)(2,1)S(1)}, u32[]{:S(2)}, u32[]{:S(2)}) collective-permute-start(bf16[64,256]{1,0:T(8,128)(2,1)} %shard_map.70), channel_id=1, source_target_pairs={{0,1},{1,0},{2,3},{3,2},{4,5},{5,4},{6,7},{7,6},{8,9},{9,8},{10,11... | collective-permute-start | bytes 98312 | tf_op jit(solution)/shard_map/ppermute | solution.py:267
  42.5 5.9 %collective-permute-start.11 = (bf16[256,256]{1,0:T(8,128)(2,1)S(1)}, bf16[256,256]{1,0:T(8,128)(2,1)S(1)}, u32[]{:S(2)}, u32[]{:S(2)}) collective-permute-start(bf16[256,256]{1,0:T(8,128)(2,1)S(1)} %pad_maximum_fusion.rest_0_), channel_id=1, source_target_pairs={{0,24},{4,28},{8,16},{12,20},{16,8},{20,12},{24,0},{28,4},{1,25},{... | collective-permute-start | bytes 393224 | tf_op jit(solution)/shard_map/ppermute | solution.py:267
  45.0 5.0 %collective-permute-start.9 = (bf16[256,256]{1,0:T(8,128)(2,1)S(1)}, bf16[256,256]{1,0:T(8,128)(2,1)S(1)}, u32[]{:S(2)}, u32[]{:S(2)}) collective-permute-start(bf16[256,256]{1,0:T(8,128)(2,1)S(1)} %pad_maximum_fusion.rest_0_), channel_id=1, source_target_pairs={{0,16},{4,20},{8,24},{12,28},{16,0},{20,4},{24,8},{28,12},{1,17},{... | collective-permute-start | bytes 393224 | tf_op jit(solution)/shard_map/ppermute | solution.py:267
  45.5 5.0 %collective-permute-start.7 = (bf16[256,256]{1,0:T(8,128)(2,1)S(1)}, bf16[256,256]{1,0:T(8,128)(2,1)S(1)}, u32[]{:S(2)}, u32[]{:S(2)}) collective-permute-start(bf16[256,256]{1,0:T(8,128)(2,1)S(1)} %pad_maximum_fusion.rest_0_), channel_id=1, source_target_pairs={{0,8},{4,12},{8,0},{12,4},{16,24},{20,28},{24,16},{28,20},{1,9},{5... | collective-permute-start | bytes 393224 | tf_op jit(solution)/shard_map/ppermute | solution.py:267
  46.1 19.9 %collective-permute-start.6 = (bf16[256,256]{1,0:T(8,128)(2,1)S(1)}, bf16[256,256]{1,0:T(8,128)(2,1)S(1)}, u32[]{:S(2)}, u32[]{:S(2)}) collective-permute-start(bf16[256,256]{1,0:T(8,128)(2,1)S(1)} %pad_maximum_fusion.rest_0_), channel_id=1, source_target_pairs={{0,4},{4,0},{8,12},{12,8},{16,20},{20,16},{24,28},{28,24},{1,5},{5... | collective-permute-start | bytes 393224 | tf_op jit(solution)/shard_map/ppermute | solution.py:267
  48.5 17.5 %collective-permute-start.12 = (bf16[256,256]{1,0:T(8,128)(2,1)S(1)}, bf16[256,256]{1,0:T(8,128)(2,1)S(1)}, u32[]{:S(2)}, u32[]{:S(2)}) collective-permute-start(bf16[256,256]{1,0:T(8,128)(2,1)S(1)} %collective-permute-done.11.rest_6_), channel_id=1, source_target_pairs={{0,4},{4,0},{8,12},{12,8},{16,20},{20,16},{24,28},{28,24},{1,5},{5... | collective-permute-start | bytes 393224 | tf_op jit(solution)/shard_map/ppermute | solution.py:267
  50.0 16.0 %collective-permute-start.10 = (bf16[256,256]{1,0:T(8,128)(2,1)S(1)}, bf16[256,256]{1,0:T(8,128)(2,1)S(1)}, u32[]{:S(2)}, u32[]{:S(2)}) collective-permute-start(bf16[256,256]{1,0:T(8,128)(2,1)S(1)} %collective-permute-done.9.rest_4_), channel_id=1, source_target_pairs={{0,4},{4,0},{8,12},{12,8},{16,20},{20,16},{24,28},{28,24},{1,5},{5... | collective-permute-start | bytes 393224 | tf_op jit(solution)/shard_map/ppermute | solution.py:267
  50.5 15.5 %collective-permute-start.8 = (bf16[256,256]{1,0:T(8,128)(2,1)S(1)}, bf16[256,256]{1,0:T(8,128)(2,1)S(1)}, u32[]{:S(2)}, u32[]{:S(2)}) collective-permute-start(bf16[256,256]{1,0:T(8,128)(2,1)S(1)} %collective-permute-done.7.rest_2_), channel_id=1, source_target_pairs={{0,4},{4,0},{8,12},{12,8},{16,20},{20,16},{24,28},{28,24},{1,5},{5... | collective-permute-start | bytes 393224 | tf_op jit(solution)/shard_map/ppermute | solution.py:267
  66.0 0.8 %copy-start = (f32[128,64]{1,0:T(8,128)S(1)}, f32[128,64]{1,0:T(8,128)}, u32[]{:S(2)}) copy-start(f32[128,64]{1,0:T(8,128)} %shard_map.68.source_ref) | copy-start | bytes 98308

commit v2 on v1

--- a/solution.py
+++ b/solution.py
@@ -10,6 +10,9 @@
 TILE = 128
 LO = 128
 EPSILON = 1e-06
+VMEM_SMALL = 8 << 20
+VMEM_SIGNATURE = 60 << 20
+VMEM_TILES = 24 << 20
 
 
 def _fits(count, most):
@@ -19,7 +22,7 @@
 
 
 def _signature_kernel(
-    docs, entries, hi_n, stride, unroll, k_step, parts,
+    first, docs, entries, hi_n, stride, unroll, k_step, parts,
     ids_ref, w_ref, proj_ref, *rest,
 ):
     out_refs = rest[:parts]
@@ -33,7 +36,7 @@
 
     for c in range(chunks):
         chunk_copy(c).start()
-    weights[...] = w_ref[...].astype(jnp.float32)
+    weights[...] = w_ref[first:first + docs, :].astype(jnp.float32)
 
     def pair(p):
         iota_hi = lax.broadcasted_iota(jnp.int32, (hi_n, entries), 0).astype(jnp.bfloat16)
@@ -43,7 +46,7 @@
         zero_lo = jnp.zeros((LO, entries), jnp.bfloat16)
         his, los = [], []
         for e in range(2):
-            ids = ids_ref[pl.ds(2 * p + e, 1), :]
+            ids = ids_ref[pl.ds(first + 2 * p + e, 1), :]
             w = weights[pl.ds(2 * p + e, 1), :].astype(jnp.bfloat16)
             hi = (ids // LO).astype(jnp.float32).astype(jnp.bfloat16)
             lo = (ids % LO).astype(jnp.float32).astype(jnp.bfloat16)
@@ -78,9 +81,9 @@
                 top = a.astype(jnp.bfloat16)
                 lhs[:docs, q * LO:(q + 1) * LO] = top
                 lhs[docs:, q * LO:(q + 1) * LO] = (a - top.astype(jnp.float32)).astype(jnp.bfloat16)
-            first = pl.multiple_of(k * k_step * LO, k_step * LO)
+            feature = pl.multiple_of(k * k_step * LO, k_step * LO)
             r = jnp.dot(
-                lhs[...], proj[c, pl.ds(first, k_step * LO), :],
+                lhs[...], proj[c, pl.ds(feature, k_step * LO), :],
                 preferred_element_type=jnp.float32,
             )
             r = r[:docs] + r[docs:]
@@ -99,17 +102,17 @@
         out_refs[k][...] = total[pl.ds(row, part_rows), :]
 
 
-def _signature_parts(ids, w, projection, parts):
-    docs, entries = ids.shape
+def _signature_parts(ids, w, projection, parts, first, docs):
+    entries = ids.shape[1]
     feats, width = projection.shape
     hi_n = feats // LO
-    chunks = 4
+    chunks = 2
     stride = docs + 8
-    k_step = _fits(hi_n // chunks, 32)
-    unroll = _fits(docs // 2, 16)
+    k_step = _fits(hi_n // chunks, 64)
+    unroll = _fits(docs // 2, 64)
     return pl.pallas_call(
         functools.partial(
-            _signature_kernel, docs, entries, hi_n, stride, unroll, k_step, parts
+            _signature_kernel, first, docs, entries, hi_n, stride, unroll, k_step, parts
         ),
         out_shape=[jax.ShapeDtypeStruct((docs // parts, width), jnp.float32)] * parts,
         in_specs=[
@@ -126,7 +129,10 @@
             pltpu.VMEM((docs, width), jnp.float32),
             pltpu.SemaphoreType.DMA((chunks,)),
         ],
-        compiler_params=pltpu.CompilerParams(vmem_limit_bytes=60 << 20),
+        compiler_params=pltpu.CompilerParams(vmem_limit_bytes=VMEM_SIGNATURE),
+        cost_estimate=pl.CostEstimate(
+            flops=6 * docs * feats * width, bytes_accessed=2 * feats * width, transcendentals=0
+        ),
     )(ids, w, projection)
 
 
@@ -144,10 +150,11 @@
         out_shape=jax.ShapeDtypeStruct(parts[0].shape, jnp.bfloat16),
         in_specs=[pl.BlockSpec(memory_space=pltpu.VMEM)] * len(parts),
         out_specs=pl.BlockSpec(memory_space=pltpu.VMEM),
+        compiler_params=pltpu.CompilerParams(vmem_limit_bytes=VMEM_SMALL),
     )(*parts)
 
 
-def _source_kernel(docs, tiles, rows_dev, shard, targets_ref, out_ref):
+def _source_kernel(docs, tiles, rows_dev, shard, targets_ref, out_ref, sums):
     me_docs = lax.axis_index("docs")
     me_feat = lax.axis_index("feat")
     sub = docs // 128
@@ -158,11 +165,11 @@
     zero_lo = jnp.zeros((TILE, 128), jnp.bfloat16)
     zero_hi = jnp.zeros((tiles, 128), jnp.bfloat16)
     lane = lax.broadcasted_iota(jnp.int32, (1, 128), 1)
-    out_ref[...] = jnp.zeros_like(out_ref)
+    sums[...] = jnp.zeros_like(sums)
 
     def step(i, _):
-        block = targets_ref[pl.ds(pl.multiple_of(i * 8, 8), 8), :] - base
-        dev = ((i * 8) // rows_dev) ^ me_docs
+        block = targets_ref[pl.ds(pl.multiple_of(i * 8, 8), 8), :].astype(jnp.int32) - base
+        dev = (i * 8) // rows_dev
         dev_row = jnp.full((tiles, 128), dev.astype(jnp.float32), jnp.float32).astype(jnp.bfloat16)
         los, his = [], []
         for r in range(8):
@@ -177,58 +184,109 @@
                 jnp.where(here, jnp.broadcast_to(place, (tiles, 128)), zero_hi),
                 jnp.where(here, dev_row, zero_hi),
             ], axis=0))
-        out_ref[...] += lax.dot_general(
+        sums[...] += lax.dot_general(
             jnp.concatenate(los, axis=1), jnp.concatenate(his, axis=1),
             (((1,), (1,)), ((), ())), preferred_element_type=jnp.float32,
         )
         return 0
 
     lax.fori_loop(0, targets_ref.shape[0] // 8, step, 0)
+    out_ref[...] = sums[:, :tiles] + sums[:, tiles:] * docs
 
 
 def _sources(targets, docs, tiles, rows_dev, shard):
     return pl.pallas_call(
         functools.partial(_source_kernel, docs, tiles, rows_dev, shard),
-        out_shape=jax.ShapeDtypeStruct((TILE, 2 * tiles), jnp.float32),
+        out_shape=jax.ShapeDtypeStruct((TILE, tiles), jnp.float32),
         in_specs=[pl.BlockSpec(memory_space=pltpu.VMEM)],
         out_specs=pl.BlockSpec(memory_space=pltpu.VMEM),
+        scratch_shapes=[pltpu.VMEM((TILE, 2 * tiles), jnp.float32)],
+        compiler_params=pltpu.CompilerParams(vmem_limit_bytes=VMEM_SMALL),
+        cost_estimate=pl.CostEstimate(
+            flops=2 * targets.size * TILE * TILE, bytes_accessed=4 * targets.size, transcendentals=0
+        ),
     )(targets)
 
 
-def _tiles_kernel(blocks, group, counts_ref, source_ref, *rest):
+def _choose(pick, source_ref, tiles, blocks, rows, period, offset):
+    lane = lax.broadcasted_iota(jnp.int32, (TILE, rows), 1).astype(jnp.bfloat16)
+    one = jnp.ones((TILE, rows), jnp.bfloat16)
+    zero = jnp.zeros((TILE, rows), jnp.bfloat16)
+    for j, t in enumerate(tiles):
+        s = jnp.broadcast_to(source_ref[:, t:t + 1], (TILE, rows))
+        for b in range(blocks):
+            here = (s - (b * period + offset)).astype(jnp.bfloat16)
+            pick[j * TILE:(j + 1) * TILE, b * rows:(b + 1) * rows] = jnp.where(lane == here, one, zero)
+
+
+def _collect(units, unit_refs):
+    rows = unit_refs[0].shape[0]
+    for b, ref in enumerate(unit_refs):
+        units[b * rows:(b + 1) * rows, :] = ref[...]
+
+
+def _place_kernel(blocks, group, period, offset, source_ref, *rest):
     unit_refs = rest[:blocks]
-    cosine_hbm, affinity_ref, cosine, sems = rest[blocks:]
+    table, units, pick = rest[blocks:]
+    rows = unit_refs[0].shape[0]
+    _collect(units, unit_refs)
+    groups = table.shape[0] // (group * TILE)
+    for g in range(-1, groups):
+        if g + 1 < groups:
+            span = range((g + 1) * group, (g + 2) * group)
+            _choose(pick.at[(g + 1) % 2], source_ref, span, blocks, rows, period, offset)
+        if g >= 0:
+            table[g * group * TILE:(g + 1) * group * TILE, :] = jnp.dot(
+                pick[g % 2], units[...], preferred_element_type=jnp.float32
+            ).astype(jnp.bfloat16)
+
+
+def _place(source, units, period, offset):
+    tiles = source.shape[1]
+    group = _fits(tiles, 4)
+    rows, width = units[0].shape
+    return pl.pallas_call(
+        functools.partial(_place_kernel, len(units), group, period, offset),
+        out_shape=jax.ShapeDtypeStruct((tiles * TILE, width), jnp.bfloat16),
+        in_specs=[pl.BlockSpec(memory_space=pltpu.VMEM)] * (1 + len(units)),
+        out_specs=pl.BlockSpec(memory_space=pltpu.VMEM),
+        scratch_shapes=[
+            pltpu.VMEM((len(units) * rows, width), jnp.bfloat16),
+            pltpu.VMEM((2, group * TILE, len(units) * rows), jnp.bfloat16),
+        ],
+        compiler_params=pltpu.CompilerParams(vmem_limit_bytes=VMEM_TILES),
+        cost_estimate=pl.CostEstimate(
+            flops=2 * tiles * TILE * width * len(units) * rows,
+            bytes_accessed=2 * tiles * TILE * width, transcendentals=0,
+        ),
+    )(source, *units)
+
+
+def _tiles_kernel(blocks, group, period, offset, has_placed, counts_ref, source_ref, *rest):
+    unit_refs = rest[:blocks]
+    placed_ref = rest[blocks] if has_placed else None
+    cosine_hbm, affinity_ref, cosine, units, pick, table, sems = rest[blocks + has_placed:]
     tiles = cosine.shape[0]
-    docs = unit_refs[0].shape[0]
-    lane = lax.broadcasted_iota(jnp.int32, (TILE, docs), 1).astype(jnp.bfloat16)
-    one = jnp.ones((TILE, docs), jnp.bfloat16)
-    zero = jnp.zeros((TILE, docs), jnp.bfloat16)
+    rows = unit_refs[0].shape[0]
     row_of = lax.broadcasted_iota(jnp.int32, (TILE, TILE), 0)
     col_of = lax.broadcasted_iota(jnp.int32, (TILE, TILE), 1)
-    place = source_ref[:, :tiles] + source_ref[:, tiles:] * docs
+    _collect(units, unit_refs)
 
     def copy_out(g):
         span = pl.ds(g * group, group)
         return pltpu.make_async_copy(cosine.at[span], cosine_hbm.at[span], sems.at[g])
 
-    for g in range(tiles // group):
-        total = jnp.zeros((group * TILE, unit_refs[0].shape[1]), jnp.float32)
-        sources = [
-            jnp.broadcast_to(place[:, t:t + 1], (TILE, docs))
-            for t in range(g * group, (g + 1) * group)
-        ]
-        for b in range(blocks):
-            pick = jnp.concatenate([
-                jnp.where(lane == (s - b * docs).astype(jnp.bfloat16), one, zero) for s in sources
-            ], axis=0)
-            total = total + jnp.dot(pick, unit_refs[b][...], preferred_element_type=jnp.float32)
-        table = total.astype(jnp.bfloat16)
-        for j in range(group):
-            t = g * group + j
-            rows = table[j * TILE:(j + 1) * TILE]
+    def place(g):
+        span = slice(g * group * TILE, (g + 1) * group * TILE)
+        new = jnp.dot(pick[g % 2], units[...], preferred_element_type=jnp.float32).astype(jnp.bfloat16)
+        table[span, :] = new + placed_ref[span, :] if has_placed else new
+
+    def multiply(g):
+        for t in range(g * group, (g + 1) * group):
+            slots = table[t * TILE:(t + 1) * TILE, :]
             filled = counts_ref[t, 0]
             products = lax.dot_general(
-                rows, rows, (((1,), (1,)), ((), ())), preferred_element_type=jnp.float32
+                slots, slots, (((1,), (1,)), ((), ())), preferred_element_type=jnp.float32
             )
             products = jnp.where(jnp.maximum(row_of, col_of) < filled, products, 0.0)
             cosine[t] = products
@@ -236,28 +294,47 @@
             divisor = jnp.full((1, TILE), jnp.maximum(filled - 1, 1).astype(jnp.float32))
             affinity_ref[t:t + 1, :] = others / divisor
         copy_out(g).start()
-    for g in range(tiles // group):
+
+    groups = tiles // group
+    for g in range(-1, groups + 1):
+        if g + 1 < groups:
+            span = range((g + 1) * group, (g + 2) * group)
+            _choose(pick.at[(g + 1) % 2], source_ref, span, blocks, rows, period, offset)
+        if 0 <= g < groups:
+            place(g)
+        if g >= 1:
+            multiply(g - 1)
+    for g in range(groups):
         copy_out(g).wait()
 
 
-def _tiles(counts, source, units):
+def _tiles(counts, source, units, placed, period, offset):
     tiles = counts.shape[0]
     group = _fits(tiles, 4)
-    return pl.pallas_call(
-        functools.partial(_tiles_kernel, len(units), group),
+    rows, width = units[0].shape
+    extra = [] if placed is None else [placed]
+    return pl.pallas_call(
+        functools.partial(_tiles_kernel, len(units), group, period, offset, len(extra)),
         out_shape=[
             jax.ShapeDtypeStruct((tiles, TILE, TILE), jnp.float32),
             jax.ShapeDtypeStruct((tiles, TILE), jnp.float32),
         ],
         in_specs=[pl.BlockSpec(memory_space=pltpu.SMEM)]
-        + [pl.BlockSpec(memory_space=pltpu.VMEM)] * (1 + len(units)),
+        + [pl.BlockSpec(memory_space=pltpu.VMEM)] * (1 + len(units) + len(extra)),
         out_specs=[pl.BlockSpec(memory_space=pl.ANY), pl.BlockSpec(memory_space=pltpu.VMEM)],
         scratch_shapes=[
             pltpu.VMEM((tiles, TILE, TILE), jnp.float32),
+            pltpu.VMEM((len(units) * rows, width), jnp.bfloat16),
+            pltpu.VMEM((2, group * TILE, len(units) * rows), jnp.bfloat16),
+            pltpu.VMEM((tiles * TILE, width), jnp.bfloat16),
             pltpu.SemaphoreType.DMA((tiles // group,)),
         ],
-        compiler_params=pltpu.CompilerParams(vmem_limit_bytes=48 << 20),
-    )(counts, source, *units)
+        compiler_params=pltpu.CompilerParams(vmem_limit_bytes=VMEM_TILES),
+        cost_estimate=pl.CostEstimate(
+            flops=2 * tiles * TILE * width * (len(units) * rows + TILE),
+            bytes_accessed=4 * tiles * TILE * TILE, transcendentals=0,
+        ),
+    )(counts, source, *units, *extra)
 
 
 def solution(mesh):
@@ -265,24 +342,33 @@
 
     def send(x, axis, size, k):
         return lax.ppermute(x, axis, [(i, i ^ k) for i in range(size)])
+
+    def everywhere(x, axis, size, step):
+        return [x] + [send(x, axis, size, k) for k in range(step, size, step)]
 
     def per_device(ids, w, projection, lists, counts):
         docs = ids.shape[0]
         tiles = counts.shape[0]
         shard = docs // n_feat
-        targets = (lists[:, :, 0] * (tiles * TILE) + lists[:, :, 1]).T.reshape(-1, 128)
-        rows_dev = targets.shape[0]
-        targets = lax.all_gather(targets, "docs", axis=0, tiled=True)
-        parts = _signature_parts(ids, w, projection, n_feat)
-        received = [send(parts[k], "feat", n_feat, k) for k in range(1, n_feat)]
+
+        def targets_of(block):
+            return (block[:, :, 0] * (tiles * TILE) + block[:, :, 1]).T.reshape(-1, 128)
+
+        near = everywhere(targets_of(lists), "docs", n_docs, 2)
+        own = _signature_parts(ids, w, projection, n_feat, 0, docs)
+        near, own = lax.optimization_barrier((near, own))
+        received = [send(own[k], "feat", n_feat, k) for k in range(1, n_feat)]
+        near = jnp.stack(near)
+        rows_dev = near.shape[1]
+        targets = jnp.stack([near, send(near, "docs", n_docs, 1)], axis=1).reshape(-1, 128)
         source = _sources(targets, docs, tiles, rows_dev, shard)
-        own = _unit([parts[0]] + received)
-        own = jnp.concatenate([own] + [send(own, "feat", n_feat, k) for k in range(1, n_feat)])
-        near = [own] + [send(own, "docs", n_docs, k) for k in range(2, n_docs, 2)]
-        units = []
-        for block in near:
-            units += [block, send(block, "docs", n_docs, 1)]
-        cosine, affinity = _tiles(counts, source, units)
+        terms = [own[0] + received[0]] + received[1:]
+        terms, source = lax.optimization_barrier((terms, source))
+        unit = jnp.concatenate(everywhere(_unit(terms), "feat", n_feat, 1))
+        near = everywhere(unit, "docs", n_docs, 2)
+        units = [u for x in near for u in (x, send(x, "docs", n_docs, 1))]
+        placed = _place(source, units[:2], docs, 0)
+        cosine, affinity = _tiles(counts, source, units[2:], placed, docs, 2 * docs)
         return cosine[:, None], affinity[:, None]
 
     placed = (

time: 79.7 us -> 59.6 us (0.75)
  blocking collectives: 10.4 us -> 0 us
  Pallas kernels: 38.9 us -> 29.8 us
  starting transfers between devices: 13.7 us -> 17.8 us
  waiting for transfers between devices: 13.1 us -> 9.81 us
    all_gather x1 -> x0, blocking collectives: 10.4 us -> none  [per_device(): targets = lax.all_gather(targets, 'docs', axis=0, tiled=True)]
    pallas_call x2 -> x3, Pallas kernels: 32.2 us -> 25.8 us  [the longest x1 18.1 us: _signature_parts(): pl.pallas_call(functools.partial(_signature_kernel, first, docs, entries,...]
    ppermute x13 -> x17, starting transfers between devices: 13.7 us -> 17.8 us  [send(): return lax.ppermute(x, axis, [(i, i ^ k) for i in range(size)])]
    ppermute x13 -> x17, waiting for transfers between devices: 13.1 us -> 9.81 us  [send(): return lax.ppermute(x, axis, [(i, i ^ k) for i in range(size)])]
    pallas_call x1, Pallas kernels: 1.64 us -> 0.1 us  [_unit(): pl.pallas_call(_unit_kernel, out_shape=jax.ShapeDtypeStruct(parts[0].shap...]
    unnamed x13 -> x5, local copies, waits for them, and re-layouts: 1.55 us -> 0.1 us
    pallas_call x1, Pallas kernels: 5.06 us -> 3.86 us  [_sources(): pl.pallas_call(functools.partial(_source_kernel, docs, tiles, rows_dev, s...]
  transfers between devices with their start and end apart: 13 -> 17, of which waited for: 7 -> 6; matrix products, arithmetic and copies ran while one was open for 0% -> 0% of each run, Pallas kernels for 6% -> 39%
where the time goes in v2:
time: 59.6 us; the launch traced here: 59.3 us
  Pallas kernels  29.8 us (50%)
  starting transfers between devices  17.8 us (30%)
  waiting for transfers between devices  9.81 us (16%)
  between operations  0.96 us (2%)
  local copies, waits for them, and re-layouts  0.91 us (2%)
    pallas_call x1, Pallas kernels, _signature_parts(): pl.pallas_call(functools.partial(_signature_kernel, first, docs, entries,...  18.1 us
    ppermute x17, starting transfers between devices, send(): return lax.ppermute(x, axis, [(i, i ^ k) for i in range(size)])  17.8 us
    ppermute x17, waiting for transfers between devices, send(): return lax.ppermute(x, axis, [(i, i ^ k) for i in range(size)])  9.81 us
    pallas_call x1, Pallas kernels, _tiles(): pl.pallas_call(functools.partial(_tiles_kernel, len(units), group, period...  6.38 us
    pallas_call x1, Pallas kernels, _sources(): pl.pallas_call(functools.partial(_source_kernel, docs, tiles, rows_dev, s...  3.86 us
    pallas_call x1, Pallas kernels, _place(): pl.pallas_call(functools.partial(_place_kernel, len(units), group, period...  1.35 us
  transfers between devices with their start and end apart: 17, of which 6 were waited for; matrix products, arithmetic and copies ran while one was open for 0% of the time, Pallas kernels for 39%

profile of v2, /device:TPU:0, one launch (start us, length us, event | category | flops | bytes accessed | tf_op | source)
XLA Modules:
  0.0 59.3 jit_solution(17680523668471552536)
XLA Ops:
  0.6 0.8 %fusion.2 = (s32[256,8,1]{0,2,1:T(1,128)S(1)}, s32[256,8,1]{0,2,1:T(1,128)S(1)}) fusion(s32[256,8,2]{0,2,1:T(2,128)} %param.8), kind=kLoop, calls=%fused_computation.7 | loop fusion | bytes 32768 | tf_op jit(solution)/shard_map/slice | solution.py:355
  1.5 4.0 %collective-permute-start.2 = (s32[16,128]{1,0:T(8,128)S(1)}, s32[16,128]{1,0:T(8,128)S(1)}, u32[]{:S(2)}, u32[]{:S(2)}) collective-permute-start(s32[16,128]{1,0:T(8,128)S(1)} %reshape.13), channel_id=1, source_target_pairs={{0,24},{4,28},{8,16},{12,20},{16,8},{20,12},{24,0},{28,4},{1,25},{... | collective-permute-start | bytes 24584 | tf_op jit(solution)/shard_map/ppermute | solution.py:344
  5.4 0.5 collective-permute-start.1
  5.9 0.1 collective-permute-start
  6.1 18.1 %shard_map.68 = (f32[64,256]{1,0:T(8,128)}, f32[64,256]{1,0:T(8,128)}, f32[64,256]{1,0:T(8,128)}, f32[64,256]{1,0:T(8,128)}) custom-call(s32[256,128]{1,0:T(8,128)} %ids_ref.1, bf16[256,128]{1,0:T(8,128)(2,1)} %w_ref.1, bf16[32768,256]{1,0:T(8,128)(2,1)} %proj_ref.1), custom_call_target="tpu_custom_call" | custom-call | flops 12884901888 | bytes 16777216 | tf_op jit(solution)/shard_map/pallas_call | solution.py:113
  24.1 0.0 copy-start
  24.2 0.0 copy-start.1
  24.2 0.0 collective-permute-done.1
  24.2 0.1 collective-permute-start.6
  24.3 2.0 %collective-permute-start.3 = (f32[64,256]{1,0:T(8,128)}, f32[64,256]{1,0:T(8,128)S(1)}, u32[]{:S(2)}, u32[]{:S(2)}) collective-permute-start(f32[64,256]{1,0:T(8,128)} %get-tuple-element.25), channel_id=1, source_target_pairs={{0,1},{1,0},{2,3},{3,2},{4,5},{5,4},{6,7},{7,6},{8,9},{9,8},{10,11... | collective-permute-start | bytes 196616 | tf_op jit(solution)/shard_map/ppermute | solution.py:344
  26.3 2.6 %collective-permute-start.4 = (f32[64,256]{1,0:T(8,128)}, f32[64,256]{1,0:T(8,128)S(1)}, u32[]{:S(2)}, u32[]{:S(2)}) collective-permute-start(f32[64,256]{1,0:T(8,128)} %get-tuple-element.26), channel_id=1, source_target_pairs={{0,2},{1,3},{2,0},{3,1},{4,6},{5,7},{6,4},{7,5},{8,10},{9,11},{10,... | collective-permute-start | bytes 196616 | tf_op jit(solution)/shard_map/ppermute | solution.py:344
  28.9 0.0 collective-permute-start.5
  28.9 0.0 collective-permute-done.6
  28.9 3.9 %shard_map.69.source_ref = f32[128,32]{1,0:T(8,128)S(1)} custom-call(s32[128,128]{1,0:T(8,128)S(1)} %bitcast.20), custom_call_target="tpu_custom_call" | custom-call | flops 536870912 | bytes 65536 | tf_op jit(solution)/shard_map/pallas_call | solution.py:198
  32.8 1.4 %collective-permute-done.4.refs_1_ = f32[64,256]{1,0:T(8,128)S(1)} collective-permute-done((f32[64,256]{1,0:T(8,128)}, f32[64,256]{1,0:T(8,128)S(1)}, u32[]{:S(2)}, u32[]{:S(2)}) %collective-permute-start.4) | collective-permute-done | bytes 65568 | tf_op jit(solution)/shard_map/ppermute | solution.py:344
  34.3 1.0 %collective-permute-done.5.refs_2_ = f32[64,256]{1,0:T(8,128)S(1)} collective-permute-done((f32[64,256]{1,0:T(8,128)}, f32[64,256]{1,0:T(8,128)S(1)}, u32[]{:S(2)}, u32[]{:S(2)}) %collective-permute-start.5) | collective-permute-done | bytes 65568 | tf_op jit(solution)/shard_map/ppermute | solution.py:344
  35.3 0.1 shard_map.70
  35.4 2.4 %collective-permute-start.9 = (bf16[64,256]{1,0:T(8,128)(2,1)S(1)}, bf16[64,256]{1,0:T(8,128)(2,1)S(1)}, u32[]{:S(2)}, u32[]{:S(2)}) collective-permute-start(bf16[64,256]{1,0:T(8,128)(2,1)S(1)} %shard_map.70), channel_id=1, source_target_pairs={{0,3},{1,2},{2,1},{3,0},{4,7},{5,6},{6,5},{7,4},{8,11},{9,10},{10,... | collective-permute-start | bytes 98312 | tf_op jit(solution)/shard_map/ppermute | solution.py:344
  37.8 0.3 collective-permute-start.8
  38.1 1.7 %collective-permute-start.7 = (bf16[64,256]{1,0:T(8,128)(2,1)S(1)}, bf16[64,256]{1,0:T(8,128)(2,1)S(1)}, u32[]{:S(2)}, u32[]{:S(2)}) collective-permute-start(bf16[64,256]{1,0:T(8,128)(2,1)S(1)} %shard_map.70), channel_id=1, source_target_pairs={{0,1},{1,0},{2,3},{3,2},{4,5},{5,4},{6,7},{7,6},{8,9},{9,8},{10,11... | collective-permute-start | bytes 98312 | tf_op jit(solution)/shard_map/ppermute | solution.py:344
  39.8 1.6 %collective-permute-done.9 = bf16[64,256]{1,0:T(8,128)(2,1)S(1)} collective-permute-done((bf16[64,256]{1,0:T(8,128)(2,1)S(1)}, bf16[64,256]{1,0:T(8,128)(2,1)S(1)}, u32[]{:S(2)}, u32[]{:S(2)}) %collective-permute-start.9) | collective-permute-done | bytes 32800 | tf_op jit(solution)/shard_map/ppermute | solution.py:344
  41.4 1.4 %collective-permute-done.8 = bf16[64,256]{1,0:T(8,128)(2,1)S(1)} collective-permute-done((bf16[64,256]{1,0:T(8,128)(2,1)S(1)}, bf16[64,256]{1,0:T(8,128)(2,1)S(1)}, u32[]{:S(2)}, u32[]{:S(2)}) %collective-permute-start.8) | collective-permute-done | bytes 32800 | tf_op jit(solution)/shard_map/ppermute | solution.py:344
  42.7 0.0 collective-permute-done.7
  42.8 2.5 %collective-permute-start.14 = (bf16[256,256]{1,0:T(8,128)(2,1)S(1)}, bf16[256,256]{1,0:T(8,128)(2,1)S(1)}, u32[]{:S(2)}, u32[]{:S(2)}) collective-permute-start(bf16[256,256]{1,0:T(8,128)(2,1)S(1)} %pad_maximum_fusion.rest_0_), channel_id=1, source_target_pairs={{0,24},{4,28},{8,16},{12,20},{16,8},{20,12},{24,0},{28,4},{1,25},{... | collective-permute-start | bytes 393224 | tf_op jit(solution)/shard_map/ppermute | solution.py:344
  45.3 0.5 collective-permute-start.12
  45.8 0.5 collective-permute-start.10
  46.3 3.1 %collective-permute-done.14.rest_4_ = bf16[256,256]{1,0:T(8,128)(2,1)S(1)} collective-permute-done((bf16[256,256]{1,0:T(8,128)(2,1)S(1)}, bf16[256,256]{1,0:T(8,128)(2,1)S(1)}, u32[]{:S(2)}, u32[]{:S(2)}) %collective-permute-start.14) | collective-permute-done | bytes 131104 | tf_op jit(solution)/shard_map/ppermute | solution.py:344
  49.4 1.3 %collective-permute-done.12.rest_2_ = bf16[256,256]{1,0:T(8,128)(2,1)S(1)} collective-permute-done((bf16[256,256]{1,0:T(8,128)(2,1)S(1)}, bf16[256,256]{1,0:T(8,128)(2,1)S(1)}, u32[]{:S(2)}, u32[]{:S(2)}) %collective-permute-start.12) | collective-permute-done | bytes 131104 | tf_op jit(solution)/shard_map/ppermute | solution.py:344
  50.8 0.5 collective-permute-start.11
  51.3 0.1 copy.14.counts_ref
  51.4 1.3 %shard_map.71.rest_6_ = bf16[4096,256]{1,0:T(8,128)(2,1)S(1)} custom-call(f32[128,32]{1,0:T(8,128)S(1)} %shard_map.69.source_ref, bf16[256,256]{1,0:T(8,128)(2,1)S(1)} %pad_maximum_fusion.rest_0_, bf16[256,256]{1,0:T(8,128)(2,1)S(1)} %collective-permute-done.16.rest_1_), custom_call_target="tpu_custom_call" | custom-call | flops 1073741824 | bytes 2097152 | tf_op jit(solution)/shard_map/pallas_call | solution.py:248
  52.8 6.4 %shard_map.72 = (f32[32,128,128]{2,1,0:T(8,128)}, f32[32,128]{1,0:T(8,128)}) custom-call(s32[32,1]{1,0:T(8,128)S(1)} %copy.14.counts_ref, f32[128,32]{1,0:T(8,128)S(1)} %shard_map.69.source_ref, bf16[256,256]{1,0:T(8,128)(2,1)S(1)} %collective-permute-done.10.rest_0_, bf16[256,256]{1,0:T(8,128)(2,1)S(1)} %collective-permute-done.11.rest_1_, ...), custom_call_target="tpu_custom_call" | custom-call | flops 3489660928 | bytes 2097152 | tf_op jit(solution)/shard_map/pallas_call | solution.py:316
  (19 shorter events, 0.1 us)
Async XLA Ops:
  1.5 22.7 %collective-permute-start.2 = (s32[16,128]{1,0:T(8,128)S(1)}, s32[16,128]{1,0:T(8,128)S(1)}, u32[]{:S(2)}, u32[]{:S(2)}) collective-permute-start(s32[16,128]{1,0:T(8,128)S(1)} %reshape.13), channel_id=1, source_target_pairs={{0,24},{4,28},{8,16},{12,20},{16,8},{20,12},{24,0},{28,4},{1,25},{... | collective-permute-start | bytes 24584 | tf_op jit(solution)/shard_map/ppermute | solution.py:344
  5.4 18.8 %collective-permute-start.1 = (s32[16,128]{1,0:T(8,128)S(1)}, s32[16,128]{1,0:T(8,128)S(1)}, u32[]{:S(2)}, u32[]{:S(2)}) collective-permute-start(s32[16,128]{1,0:T(8,128)S(1)} %reshape.13), channel_id=1, source_target_pairs={{0,16},{4,20},{8,24},{12,28},{16,0},{20,4},{24,8},{28,12},{1,17},{... | collective-permute-start | bytes 24584 | tf_op jit(solution)/shard_map/ppermute | solution.py:344
  5.9 18.3 %collective-permute-start = (s32[16,128]{1,0:T(8,128)S(1)}, s32[16,128]{1,0:T(8,128)S(1)}, u32[]{:S(2)}, u32[]{:S(2)}) collective-permute-start(s32[16,128]{1,0:T(8,128)S(1)} %reshape.13), channel_id=1, source_target_pairs={{0,8},{4,12},{8,0},{12,4},{16,24},{20,28},{24,16},{28,20},{1,9},{5... | collective-permute-start | bytes 24584 | tf_op jit(solution)/shard_map/ppermute | solution.py:344
  24.1 8.7 %copy-start = (f32[64,256]{1,0:T(8,128)S(1)}, f32[64,256]{1,0:T(8,128)}, u32[]{:S(2)}) copy-start(f32[64,256]{1,0:T(8,128)} %get-tuple-element.24) | copy-start | bytes 196612
  24.2 27.1 %copy-start.1 = (s32[32,1]{0,1:T(1,128)S(1)}, s32[32,1]{0,1:T(1,128)}, u32[]{:S(2)}) copy-start(s32[32,1]{0,1:T(1,128)} %param.9) | copy-start | bytes 388
  24.2 4.7 %collective-permute-start.6 = (s32[4,16,128]{2,1,0:T(8,128)S(1)}, s32[4,16,128]{2,1,0:T(8,128)S(1)}, u32[]{:S(2)}, u32[]{:S(2)}) collective-permute-start(s32[4,16,128]{2,1,0:T(8,128)S(1)} %get-tuple-element.43), channel_id=1, source_target_pairs={{0,4},{4,0},{8,12},{12,8},{16,20},{20,16},{24,28},{28,24},{1,5},{5... | collective-permute-start | bytes 98312 | tf_op jit(solution)/shard_map/ppermute | solution.py:344
  24.3 8.5 %collective-permute-start.3 = (f32[64,256]{1,0:T(8,128)}, f32[64,256]{1,0:T(8,128)S(1)}, u32[]{:S(2)}, u32[]{:S(2)}) collective-permute-start(f32[64,256]{1,0:T(8,128)} %get-tuple-element.25), channel_id=1, source_target_pairs={{0,1},{1,0},{2,3},{3,2},{4,5},{5,4},{6,7},{7,6},{8,9},{9,8},{10,11... | collective-permute-start | bytes 196616 | tf_op jit(solution)/shard_map/ppermute | solution.py:344
  26.3 7.9 %collective-permute-start.4 = (f32[64,256]{1,0:T(8,128)}, f32[64,256]{1,0:T(8,128)S(1)}, u32[]{:S(2)}, u32[]{:S(2)}) collective-permute-start(f32[64,256]{1,0:T(8,128)} %get-tuple-element.26), channel_id=1, source_target_pairs={{0,2},{1,3},{2,0},{3,1},{4,6},{5,7},{6,4},{7,5},{8,10},{9,11},{10,... | collective-permute-start | bytes 196616 | tf_op jit(solution)/shard_map/ppermute | solution.py:344
  28.9 6.3 %collective-permute-start.5 = (f32[64,256]{1,0:T(8,128)}, f32[64,256]{1,0:T(8,128)S(1)}, u32[]{:S(2)}, u32[]{:S(2)}) collective-permute-start(f32[64,256]{1,0:T(8,128)} %get-tuple-element.27), channel_id=1, source_target_pairs={{0,3},{1,2},{2,1},{3,0},{4,7},{5,6},{6,5},{7,4},{8,11},{9,10},{10,... | collective-permute-start | bytes 196616 | tf_op jit(solution)/shard_map/ppermute | solution.py:344
  35.4 6.0 %collective-permute-start.9 = (bf16[64,256]{1,0:T(8,128)(2,1)S(1)}, bf16[64,256]{1,0:T(8,128)(2,1)S(1)}, u32[]{:S(2)}, u32[]{:S(2)}) collective-permute-start(bf16[64,256]{1,0:T(8,128)(2,1)S(1)} %shard_map.70), channel_id=1, source_target_pairs={{0,3},{1,2},{2,1},{3,0},{4,7},{5,6},{6,5},{7,4},{8,11},{9,10},{10,... | collective-permute-start | bytes 98312 | tf_op jit(solution)/shard_map/ppermute | solution.py:344
  37.8 5.0 %collective-permute-start.8 = (bf16[64,256]{1,0:T(8,128)(2,1)S(1)}, bf16[64,256]{1,0:T(8,128)(2,1)S(1)}, u32[]{:S(2)}, u32[]{:S(2)}) collective-permute-start(bf16[64,256]{1,0:T(8,128)(2,1)S(1)} %shard_map.70), channel_id=1, source_target_pairs={{0,2},{1,3},{2,0},{3,1},{4,6},{5,7},{6,4},{7,5},{8,10},{9,11},{10,... | collective-permute-start | bytes 98312 | tf_op jit(solution)/shard_map/ppermute | solution.py:344
  38.1 4.6 %collective-permute-start.7 = (bf16[64,256]{1,0:T(8,128)(2,1)S(1)}, bf16[64,256]{1,0:T(8,128)(2,1)S(1)}, u32[]{:S(2)}, u32[]{:S(2)}) collective-permute-start(bf16[64,256]{1,0:T(8,128)(2,1)S(1)} %shard_map.70), channel_id=1, source_target_pairs={{0,1},{1,0},{2,3},{3,2},{4,5},{5,4},{6,7},{7,6},{8,9},{9,8},{10,11... | collective-permute-start | bytes 98312 | tf_op jit(solution)/shard_map/ppermute | solution.py:344
  42.8 6.7 %collective-permute-start.14 = (bf16[256,256]{1,0:T(8,128)(2,1)S(1)}, bf16[256,256]{1,0:T(8,128)(2,1)S(1)}, u32[]{:S(2)}, u32[]{:S(2)}) collective-permute-start(bf16[256,256]{1,0:T(8,128)(2,1)S(1)} %pad_maximum_fusion.rest_0_), channel_id=1, source_target_pairs={{0,24},{4,28},{8,16},{12,20},{16,8},{20,12},{24,0},{28,4},{1,25},{... | collective-permute-start | bytes 393224 | tf_op jit(solution)/shard_map/ppermute | solution.py:344
  45.3 5.5 %collective-permute-start.12 = (bf16[256,256]{1,0:T(8,128)(2,1)S(1)}, bf16[256,256]{1,0:T(8,128)(2,1)S(1)}, u32[]{:S(2)}, u32[]{:S(2)}) collective-permute-start(bf16[256,256]{1,0:T(8,128)(2,1)S(1)} %pad_maximum_fusion.rest_0_), channel_id=1, source_target_pairs={{0,16},{4,20},{8,24},{12,28},{16,0},{20,4},{24,8},{28,12},{1,17},{... | collective-permute-start | bytes 393224 | tf_op jit(solution)/shard_map/ppermute | solution.py:344
  45.8 5.0 %collective-permute-start.10 = (bf16[256,256]{1,0:T(8,128)(2,1)S(1)}, bf16[256,256]{1,0:T(8,128)(2,1)S(1)}, u32[]{:S(2)}, u32[]{:S(2)}) collective-permute-start(bf16[256,256]{1,0:T(8,128)(2,1)S(1)} %pad_maximum_fusion.rest_0_), channel_id=1, source_target_pairs={{0,8},{4,12},{8,0},{12,4},{16,24},{20,28},{24,16},{28,20},{1,9},{5... | collective-permute-start | bytes 393224 | tf_op jit(solution)/shard_map/ppermute | solution.py:344
  46.3 5.1 %collective-permute-start.16 = (bf16[256,256]{1,0:T(8,128)(2,1)S(1)}, bf16[256,256]{1,0:T(8,128)(2,1)S(1)}, u32[]{:S(2)}, u32[]{:S(2)}) collective-permute-start(bf16[256,256]{1,0:T(8,128)(2,1)S(1)} %pad_maximum_fusion.rest_0_), channel_id=1, source_target_pairs={{0,4},{4,0},{8,12},{12,8},{16,20},{20,16},{24,28},{28,24},{1,5},{5... | collective-permute-start | bytes 393224 | tf_op jit(solution)/shard_map/ppermute | solution.py:344
  49.4 3.3 %collective-permute-start.15 = (bf16[256,256]{1,0:T(8,128)(2,1)S(1)}, bf16[256,256]{1,0:T(8,128)(2,1)S(1)}, u32[]{:S(2)}, u32[]{:S(2)}) collective-permute-start(bf16[256,256]{1,0:T(8,128)(2,1)S(1)} %collective-permute-done.14.rest_4_), channel_id=1, source_target_pairs={{0,4},{4,0},{8,12},{12,8},{16,20},{20,16},{24,28},{28,24},{1,5},{5... | collective-permute-start | bytes 393224 | tf_op jit(solution)/shard_map/ppermute | solution.py:344
  50.8 2.0 %collective-permute-start.13 = (bf16[256,256]{1,0:T(8,128)(2,1)S(1)}, bf16[256,256]{1,0:T(8,128)(2,1)S(1)}, u32[]{:S(2)}, u32[]{:S(2)}) collective-permute-start(bf16[256,256]{1,0:T(8,128)(2,1)S(1)} %collective-permute-done.12.rest_2_), channel_id=1, source_target_pairs={{0,4},{4,0},{8,12},{12,8},{16,20},{20,16},{24,28},{28,24},{1,5},{5... | collective-permute-start | bytes 393224 | tf_op jit(solution)/shard_map/ppermute | solution.py:344
  50.8 2.0 %collective-permute-start.11 = (bf16[256,256]{1,0:T(8,128)(2,1)S(1)}, bf16[256,256]{1,0:T(8,128)(2,1)S(1)}, u32[]{:S(2)}, u32[]{:S(2)}) collective-permute-start(bf16[256,256]{1,0:T(8,128)(2,1)S(1)} %collective-permute-done.10.rest_0_), channel_id=1, source_target_pairs={{0,4},{4,0},{8,12},{12,8},{16,20},{20,16},{24,28},{28,24},{1,5},{5... | collective-permute-start | bytes 393224 | tf_op jit(solution)/shard_map/ppermute | solution.py:344

commit v3 on v2

--- a/solution.py
+++ b/solution.py
@@ -154,7 +154,7 @@
     )(*parts)
 
 
-def _source_kernel(docs, tiles, rows_dev, shard, targets_ref, out_ref, sums):
+def _source_kernel(docs, tiles, rows_dev, shard, step_rows, targets_ref, out_ref, sums, los, his):
     me_docs = lax.axis_index("docs")
     me_feat = lax.axis_index("feat")
     sub = docs // 128
@@ -168,39 +168,41 @@
     sums[...] = jnp.zeros_like(sums)
 
     def step(i, _):
-        block = targets_ref[pl.ds(pl.multiple_of(i * 8, 8), 8), :].astype(jnp.int32) - base
-        dev = (i * 8) // rows_dev
-        dev_row = jnp.full((tiles, 128), dev.astype(jnp.float32), jnp.float32).astype(jnp.bfloat16)
-        los, his = [], []
-        for r in range(8):
+        block = targets_ref[pl.ds(pl.multiple_of(i * step_rows, 8), step_rows), :] - base
+        for r in range(step_rows):
+            span = slice(r * 128, (r + 1) * 128)
+            dev = ((i * step_rows + r) // rows_dev).astype(jnp.float32)
+            dev_row = jnp.full((tiles, 128), dev, jnp.float32).astype(jnp.bfloat16)
             row = block[r:r + 1, :]
             hi = (row >> 7).astype(jnp.float32).astype(jnp.bfloat16)
             lo = (row & 127).astype(jnp.float32).astype(jnp.bfloat16)
             place = ((r % sub) * 128 + lane) ^ (me_feat * shard)
             place = place.astype(jnp.float32).astype(jnp.bfloat16)
-            los.append(jnp.where(iota_lo == lo, one_lo, zero_lo))
+            los[:, span] = jnp.where(iota_lo == lo, one_lo, zero_lo)
             here = iota_hi == hi
-            his.append(jnp.concatenate([
-                jnp.where(here, jnp.broadcast_to(place, (tiles, 128)), zero_hi),
-                jnp.where(here, dev_row, zero_hi),
-            ], axis=0))
+            his[:tiles, span] = jnp.where(here, jnp.broadcast_to(place, (tiles, 128)), zero_hi)
+            his[tiles:, span] = jnp.where(here, dev_row, zero_hi)
         sums[...] += lax.dot_general(
-            jnp.concatenate(los, axis=1), jnp.concatenate(his, axis=1),
-            (((1,), (1,)), ((), ())), preferred_element_type=jnp.float32,
+            los[...], his[...], (((1,), (1,)), ((), ())), preferred_element_type=jnp.float32
         )
         return 0
 
-    lax.fori_loop(0, targets_ref.shape[0] // 8, step, 0)
+    lax.fori_loop(0, targets_ref.shape[0] // step_rows, step, 0)
     out_ref[...] = sums[:, :tiles] + sums[:, tiles:] * docs
 
 
 def _sources(targets, docs, tiles, rows_dev, shard):
-    return pl.pallas_call(
-        functools.partial(_source_kernel, docs, tiles, rows_dev, shard),
+    step_rows = _fits(targets.shape[0], 32)
+    return pl.pallas_call(
+        functools.partial(_source_kernel, docs, tiles, rows_dev, shard, step_rows),
         out_shape=jax.ShapeDtypeStruct((TILE, tiles), jnp.float32),
         in_specs=[pl.BlockSpec(memory_space=pltpu.VMEM)],
         out_specs=pl.BlockSpec(memory_space=pltpu.VMEM),
-        scratch_shapes=[pltpu.VMEM((TILE, 2 * tiles), jnp.float32)],
+        scratch_shapes=[
+            pltpu.VMEM((TILE, 2 * tiles), jnp.float32),
+            pltpu.VMEM((TILE, step_rows * 128), jnp.bfloat16),
+            pltpu.VMEM((2 * tiles, step_rows * 128), jnp.bfloat16),
+        ],
         compiler_params=pltpu.CompilerParams(vmem_limit_bytes=VMEM_SMALL),
         cost_estimate=pl.CostEstimate(
             flops=2 * targets.size * TILE * TILE, bytes_accessed=4 * targets.size, transcendentals=0
@@ -354,21 +356,20 @@
         def targets_of(block):
             return (block[:, :, 0] * (tiles * TILE) + block[:, :, 1]).T.reshape(-1, 128)
 
-        near = everywhere(targets_of(lists), "docs", n_docs, 2)
         own = _signature_parts(ids, w, projection, n_feat, 0, docs)
-        near, own = lax.optimization_barrier((near, own))
         received = [send(own[k], "feat", n_feat, k) for k in range(1, n_feat)]
-        near = jnp.stack(near)
-        rows_dev = near.shape[1]
-        targets = jnp.stack([near, send(near, "docs", n_docs, 1)], axis=1).reshape(-1, 128)
+        lists, first = lax.optimization_barrier((lists, own[0] + received[0]))
+        near_lists = jnp.stack(everywhere(targets_of(lists), "docs", n_docs, 2))
+        rows_dev = near_lists.shape[1]
+        unit = jnp.concatenate(everywhere(_unit([first] + received[1:]), "feat", n_feat, 1))
+        unit, near_lists = lax.optimization_barrier((unit, near_lists))
+        far = [send(unit, "docs", n_docs, k) for k in range(2, n_docs, 2)]
+        targets = jnp.stack([near_lists, send(near_lists, "docs", n_docs, 1)], axis=1).reshape(-1, 128)
         source = _sources(targets, docs, tiles, rows_dev, shard)
-        terms = [own[0] + received[0]] + received[1:]
-        terms, source = lax.optimization_barrier((terms, source))
-        unit = jnp.concatenate(everywhere(_unit(terms), "feat", n_feat, 1))
-        near = everywhere(unit, "docs", n_docs, 2)
-        units = [u for x in near for u in (x, send(x, "docs", n_docs, 1))]
-        placed = _place(source, units[:2], docs, 0)
-        cosine, affinity = _tiles(counts, source, units[2:], placed, docs, 2 * docs)
+        placed = _place(source, [unit, send(unit, "docs", n_docs, 1)], docs, 0)
+        far, placed = lax.optimization_barrier((far, placed))
+        units = [u for x in far for u in (x, send(x, "docs", n_docs, 1))]
+        cosine, affinity = _tiles(counts, source, units, placed, docs, 2 * docs)
         return cosine[:, None], affinity[:, None]
 
     placed = (

time: 59.6 us -> 56.8 us (0.953)
  waiting for transfers between devices: 9.81 us -> 8.1 us
  Pallas kernels: 29.8 us -> 28.4 us
  other arithmetic: 0.04 us -> 0.87 us
  local copies, waits for them, and re-layouts: 0.91 us -> 0.1 us
    ppermute x17, waiting for transfers between devices: 9.81 us -> 8.1 us  [send(): return lax.ppermute(x, axis, [(i, i ^ k) for i in range(size)])]
    pallas_call x1, Pallas kernels: 3.86 us -> 2.53 us  [_sources(): pl.pallas_call(functools.partial(_source_kernel, docs, tiles, rows_dev, s...]
    add x1, other arithmetic: 0.01 us -> 0.85 us  [per_device(): lists, first = lax.optimization_barrier((lists, own[0] + received[0]))]
    slice x1 -> x0, local copies, waits for them, and re-layouts: 0.81 us -> none  [targets_of(): return (block[:, :, 0] * (tiles * TILE) + block[:, :, 1]).T.reshape(-1, 128)]
  transfers between devices with their start and end apart: 17 -> 17, of which waited for: 6 -> 9; matrix products, arithmetic and copies ran while one was open for 0% -> 2% of each run, Pallas kernels for 39% -> 7%
where the time goes in v3:
time: 56.8 us; the launch traced here: 56.7 us
  Pallas kernels  28.4 us (50%)
  starting transfers between devices  18.3 us (32%)
  waiting for transfers between devices  8.1 us (14%)
  between operations  0.89 us (2%)
  other arithmetic  0.87 us (2%)
    ppermute x17, starting transfers between devices, send(): return lax.ppermute(x, axis, [(i, i ^ k) for i in range(size)])  18.3 us
    pallas_call x1, Pallas kernels, _signature_parts(): pl.pallas_call(functools.partial(_signature_kernel, first, docs, entries,...  18.1 us
    ppermute x17, waiting for transfers between devices, send(): return lax.ppermute(x, axis, [(i, i ^ k) for i in range(size)])  8.1 us
    pallas_call x1, Pallas kernels, _tiles(): pl.pallas_call(functools.partial(_tiles_kernel, len(units), group, period...  6.38 us
    pallas_call x1, Pallas kernels, _sources(): pl.pallas_call(functools.partial(_source_kernel, docs, tiles, rows_dev, s...  2.53 us
    pallas_call x1, Pallas kernels, _place(): pl.pallas_call(functools.partial(_place_kernel, len(units), group, period...  1.35 us
  transfers between devices with their start and end apart: 17, of which 9 were waited for; matrix products, arithmetic and copies ran while one was open for 2% of the time, Pallas kernels for 7%

profile of v3, /device:TPU:0, one launch (start us, length us, event | category | flops | bytes accessed | tf_op | source)
XLA Modules:
  0.0 56.7 jit_solution(12079483935206218044)
XLA Ops:
  0.6 18.1 %shard_map.68 = (f32[64,256]{1,0:T(8,128)}, f32[64,256]{1,0:T(8,128)}, f32[64,256]{1,0:T(8,128)}, f32[64,256]{1,0:T(8,128)}) custom-call(s32[256,128]{1,0:T(8,128)} %ids_ref.1, bf16[256,128]{1,0:T(8,128)(2,1)} %w_ref.1, bf16[32768,256]{1,0:T(8,128)(2,1)} %proj_ref.1), custom_call_target="tpu_custom_call" | custom-call | flops 12884901888 | bytes 16777216 | tf_op jit(solution)/shard_map/pallas_call | solution.py:113
  18.7 3.1 %collective-permute-start = (f32[64,256]{1,0:T(8,128)}, f32[64,256]{1,0:T(8,128)S(1)}, u32[]{:S(2)}, u32[]{:S(2)}) collective-permute-start(f32[64,256]{1,0:T(8,128)} %get-tuple-element.17), channel_id=1, source_target_pairs={{0,1},{1,0},{2,3},{3,2},{4,5},{5,4},{6,7},{7,6},{8,9},{9,8},{10,11... | collective-permute-start | bytes 196616 | tf_op jit(solution)/shard_map/ppermute | solution.py:346
  21.8 2.6 %collective-permute-start.1 = (f32[64,256]{1,0:T(8,128)}, f32[64,256]{1,0:T(8,128)S(1)}, u32[]{:S(2)}, u32[]{:S(2)}) collective-permute-start(f32[64,256]{1,0:T(8,128)} %get-tuple-element.19), channel_id=1, source_target_pairs={{0,2},{1,3},{2,0},{3,1},{4,6},{5,7},{6,4},{7,5},{8,10},{9,11},{10,... | collective-permute-start | bytes 196616 | tf_op jit(solution)/shard_map/ppermute | solution.py:346
  24.4 0.0 collective-permute-start.2
  24.4 0.0 collective-permute-done
  24.4 0.9 %add.9.refs_0_ = f32[64,256]{1,0:T(8,128)S(1)} add(f32[64,256]{1,0:T(8,128)} %get-tuple-element.16, f32[64,256]{1,0:T(8,128)S(1)} %collective-permute-done) | non-fusion elementwise | flops 16384 | bytes 196608 | tf_op jit(solution)/shard_map/add | solution.py:361
  25.3 2.8 %collective-permute-start.8 = (s32[16,128]{1,0:T(8,128)S(1)}, s32[16,128]{1,0:T(8,128)S(1)}, u32[]{:S(2)}, u32[]{:S(2)}) collective-permute-start(s32[16,128]{1,0:T(8,128)S(1)} %reshape.13), channel_id=1, source_target_pairs={{0,24},{4,28},{8,16},{12,20},{16,8},{20,12},{24,0},{28,4},{1,25},{... | collective-permute-start | bytes 24584 | tf_op jit(solution)/shard_map/ppermute | solution.py:346
  28.1 0.5 collective-permute-start.7
  28.6 0.2 collective-permute-start.6
  28.9 0.4 collective-permute-done.1.refs_1_
  29.3 1.4 %collective-permute-done.2.refs_2_ = f32[64,256]{1,0:T(8,128)S(1)} collective-permute-done((f32[64,256]{1,0:T(8,128)}, f32[64,256]{1,0:T(8,128)S(1)}, u32[]{:S(2)}, u32[]{:S(2)}) %collective-permute-start.2) | collective-permute-done | bytes 65568 | tf_op jit(solution)/shard_map/ppermute | solution.py:346
  30.7 0.1 shard_map.69
  30.8 2.8 %collective-permute-start.5 = (bf16[64,256]{1,0:T(8,128)(2,1)S(1)}, bf16[64,256]{1,0:T(8,128)(2,1)S(1)}, u32[]{:S(2)}, u32[]{:S(2)}) collective-permute-start(bf16[64,256]{1,0:T(8,128)(2,1)S(1)} %shard_map.69), channel_id=1, source_target_pairs={{0,3},{1,2},{2,1},{3,0},{4,7},{5,6},{6,5},{7,4},{8,11},{9,10},{10,... | collective-permute-start | bytes 98312 | tf_op jit(solution)/shard_map/ppermute | solution.py:346
  33.6 1.7 %collective-permute-start.3 = (bf16[64,256]{1,0:T(8,128)(2,1)S(1)}, bf16[64,256]{1,0:T(8,128)(2,1)S(1)}, u32[]{:S(2)}, u32[]{:S(2)}) collective-permute-start(bf16[64,256]{1,0:T(8,128)(2,1)S(1)} %shard_map.69), channel_id=1, source_target_pairs={{0,1},{1,0},{2,3},{3,2},{4,5},{5,4},{6,7},{7,6},{8,9},{9,8},{10,11... | collective-permute-start | bytes 98312 | tf_op jit(solution)/shard_map/ppermute | solution.py:346
  35.3 1.3 %collective-permute-done.5 = bf16[64,256]{1,0:T(8,128)(2,1)S(1)} collective-permute-done((bf16[64,256]{1,0:T(8,128)(2,1)S(1)}, bf16[64,256]{1,0:T(8,128)(2,1)S(1)}, u32[]{:S(2)}, u32[]{:S(2)}) %collective-permute-start.5) | collective-permute-done | bytes 32800 | tf_op jit(solution)/shard_map/ppermute | solution.py:346
  36.6 1.8 %collective-permute-done.4 = bf16[64,256]{1,0:T(8,128)(2,1)S(1)} collective-permute-done((bf16[64,256]{1,0:T(8,128)(2,1)S(1)}, bf16[64,256]{1,0:T(8,128)(2,1)S(1)}, u32[]{:S(2)}, u32[]{:S(2)}) %collective-permute-start.4) | collective-permute-done | bytes 32800 | tf_op jit(solution)/shard_map/ppermute | solution.py:346
  38.4 0.1 collective-permute-start.9
  38.5 0.5 collective-permute-start.13
  39.0 2.4 %collective-permute-start.12 = (bf16[256,256]{1,0:T(8,128)(2,1)S(1)}, bf16[256,256]{1,0:T(8,128)(2,1)S(1)}, u32[]{:S(2)}, u32[]{:S(2)}) collective-permute-start(bf16[256,256]{1,0:T(8,128)(2,1)S(1)} %pad_maximum_fusion.rest_0_), channel_id=1, source_target_pairs={{0,24},{4,28},{8,16},{12,20},{16,8},{20,12},{24,0},{28,4},{1,25},{... | collective-permute-start | bytes 393224 | tf_op jit(solution)/shard_map/ppermute | solution.py:346
  41.4 0.5 collective-permute-start.11
  41.9 0.5 collective-permute-start.10
  42.5 2.5 %shard_map.70.source_ref = f32[128,32]{1,0:T(8,128)S(1)} custom-call(s32[128,128]{1,0:T(8,128)S(1)} %bitcast.18), custom_call_target="tpu_custom_call" | custom-call | flops 536870912 | bytes 65536 | tf_op jit(solution)/shard_map/pallas_call | solution.py:196
  45.0 1.3 %shard_map.71.rest_6_ = bf16[4096,256]{1,0:T(8,128)(2,1)S(1)} custom-call(f32[128,32]{1,0:T(8,128)S(1)} %shard_map.70.source_ref, bf16[256,256]{1,0:T(8,128)(2,1)S(1)} %pad_maximum_fusion.rest_0_, bf16[256,256]{1,0:T(8,128)(2,1)S(1)} %collective-permute-done.13.rest_1_), custom_call_target="tpu_custom_call" | custom-call | flops 1073741824 | bytes 2097152 | tf_op jit(solution)/shard_map/pallas_call | solution.py:250
  46.4 1.8 %collective-permute-done.11.rest_2_ = bf16[256,256]{1,0:T(8,128)(2,1)S(1)} collective-permute-done((bf16[256,256]{1,0:T(8,128)(2,1)S(1)}, bf16[256,256]{1,0:T(8,128)(2,1)S(1)}, u32[]{:S(2)}, u32[]{:S(2)}) %collective-permute-start.11) | collective-permute-done | bytes 131104 | tf_op jit(solution)/shard_map/ppermute | solution.py:346
  48.2 0.1 collective-permute-done.10.rest_0_
  48.3 0.5 collective-permute-start.15
  48.8 0.0 collective-permute-start.16
  48.8 0.1 copy.14.counts_ref
  48.9 0.7 %collective-permute-done.14.rest_1_ = bf16[256,256]{1,0:T(8,128)(2,1)S(1)} collective-permute-done((bf16[256,256]{1,0:T(8,128)(2,1)S(1)}, bf16[256,256]{1,0:T(8,128)(2,1)S(1)}, u32[]{:S(2)}, u32[]{:S(2)}) %collective-permute-start.14) | collective-permute-done | bytes 131104 | tf_op jit(solution)/shard_map/ppermute | solution.py:346
  49.6 0.2 collective-permute-done.15.rest_3_
  49.8 0.3 collective-permute-done.16.rest_5_
  50.1 6.4 %shard_map.72 = (f32[32,128,128]{2,1,0:T(8,128)}, f32[32,128]{1,0:T(8,128)}) custom-call(s32[32,1]{1,0:T(8,128)S(1)} %copy.14.counts_ref, f32[128,32]{1,0:T(8,128)S(1)} %shard_map.70.source_ref, bf16[256,256]{1,0:T(8,128)(2,1)S(1)} %collective-permute-done.10.rest_0_, bf16[256,256]{1,0:T(8,128)(2,1)S(1)} %collective-permute-done.14.rest_1_, ...), custom_call_target="tpu_custom_call" | custom-call | flops 3489660928 | bytes 2097152 | tf_op jit(solution)/shard_map/pallas_call | solution.py:318
  (20 shorter events, 0.1 us)
Async XLA Ops:
  0.6 24.6 %copy-start = (s32[256,8,2]{0,2,1:T(2,128)S(1)}, s32[256,8,2]{0,2,1:T(2,128)}, u32[]{:S(2)}) copy-start(s32[256,8,2]{0,2,1:T(2,128)} %param.8) | copy-start | bytes 49156
  18.7 5.7 %collective-permute-start = (f32[64,256]{1,0:T(8,128)}, f32[64,256]{1,0:T(8,128)S(1)}, u32[]{:S(2)}, u32[]{:S(2)}) collective-permute-start(f32[64,256]{1,0:T(8,128)} %get-tuple-element.17), channel_id=1, source_target_pairs={{0,1},{1,0},{2,3},{3,2},{4,5},{5,4},{6,7},{7,6},{8,9},{9,8},{10,11... | collective-permute-start | bytes 196616 | tf_op jit(solution)/shard_map/ppermute | solution.py:346
  21.8 7.5 %collective-permute-start.1 = (f32[64,256]{1,0:T(8,128)}, f32[64,256]{1,0:T(8,128)S(1)}, u32[]{:S(2)}, u32[]{:S(2)}) collective-permute-start(f32[64,256]{1,0:T(8,128)} %get-tuple-element.19), channel_id=1, source_target_pairs={{0,2},{1,3},{2,0},{3,1},{4,6},{5,7},{6,4},{7,5},{8,10},{9,11},{10,... | collective-permute-start | bytes 196616 | tf_op jit(solution)/shard_map/ppermute | solution.py:346
  24.4 6.3 %collective-permute-start.2 = (f32[64,256]{1,0:T(8,128)}, f32[64,256]{1,0:T(8,128)S(1)}, u32[]{:S(2)}, u32[]{:S(2)}) collective-permute-start(f32[64,256]{1,0:T(8,128)} %get-tuple-element.20), channel_id=1, source_target_pairs={{0,3},{1,2},{2,1},{3,0},{4,7},{5,6},{6,5},{7,4},{8,11},{9,10},{10,... | collective-permute-start | bytes 196616 | tf_op jit(solution)/shard_map/ppermute | solution.py:346
  25.3 8.3 %collective-permute-start.8 = (s32[16,128]{1,0:T(8,128)S(1)}, s32[16,128]{1,0:T(8,128)S(1)}, u32[]{:S(2)}, u32[]{:S(2)}) collective-permute-start(s32[16,128]{1,0:T(8,128)S(1)} %reshape.13), channel_id=1, source_target_pairs={{0,24},{4,28},{8,16},{12,20},{16,8},{20,12},{24,0},{28,4},{1,25},{... | collective-permute-start | bytes 24584 | tf_op jit(solution)/shard_map/ppermute | solution.py:346
  28.1 7.1 %collective-permute-start.7 = (s32[16,128]{1,0:T(8,128)S(1)}, s32[16,128]{1,0:T(8,128)S(1)}, u32[]{:S(2)}, u32[]{:S(2)}) collective-permute-start(s32[16,128]{1,0:T(8,128)S(1)} %reshape.13), channel_id=1, source_target_pairs={{0,16},{4,20},{8,24},{12,28},{16,0},{20,4},{24,8},{28,12},{1,17},{... | collective-permute-start | bytes 24584 | tf_op jit(solution)/shard_map/ppermute | solution.py:346
  28.6 6.6 %collective-permute-start.6 = (s32[16,128]{1,0:T(8,128)S(1)}, s32[16,128]{1,0:T(8,128)S(1)}, u32[]{:S(2)}, u32[]{:S(2)}) collective-permute-start(s32[16,128]{1,0:T(8,128)S(1)} %reshape.13), channel_id=1, source_target_pairs={{0,8},{4,12},{8,0},{12,4},{16,24},{20,28},{24,16},{28,20},{1,9},{5... | collective-permute-start | bytes 24584 | tf_op jit(solution)/shard_map/ppermute | solution.py:346
  30.8 5.8 %collective-permute-start.5 = (bf16[64,256]{1,0:T(8,128)(2,1)S(1)}, bf16[64,256]{1,0:T(8,128)(2,1)S(1)}, u32[]{:S(2)}, u32[]{:S(2)}) collective-permute-start(bf16[64,256]{1,0:T(8,128)(2,1)S(1)} %shard_map.69), channel_id=1, source_target_pairs={{0,3},{1,2},{2,1},{3,0},{4,7},{5,6},{6,5},{7,4},{8,11},{9,10},{10,... | collective-permute-start | bytes 98312 | tf_op jit(solution)/shard_map/ppermute | solution.py:346
  33.6 4.8 %collective-permute-start.4 = (bf16[64,256]{1,0:T(8,128)(2,1)S(1)}, bf16[64,256]{1,0:T(8,128)(2,1)S(1)}, u32[]{:S(2)}, u32[]{:S(2)}) collective-permute-start(bf16[64,256]{1,0:T(8,128)(2,1)S(1)} %shard_map.69), channel_id=1, source_target_pairs={{0,2},{1,3},{2,0},{3,1},{4,6},{5,7},{6,4},{7,5},{8,10},{9,11},{10,... | collective-permute-start | bytes 98312 | tf_op jit(solution)/shard_map/ppermute | solution.py:346
  33.6 4.8 %collective-permute-start.3 = (bf16[64,256]{1,0:T(8,128)(2,1)S(1)}, bf16[64,256]{1,0:T(8,128)(2,1)S(1)}, u32[]{:S(2)}, u32[]{:S(2)}) collective-permute-start(bf16[64,256]{1,0:T(8,128)(2,1)S(1)} %shard_map.69), channel_id=1, source_target_pairs={{0,1},{1,0},{2,3},{3,2},{4,5},{5,4},{6,7},{7,6},{8,9},{9,8},{10,11... | collective-permute-start | bytes 98312 | tf_op jit(solution)/shard_map/ppermute | solution.py:346
  38.4 4.1 %collective-permute-start.9 = (s32[4,16,128]{2,1,0:T(8,128)S(1)}, s32[4,16,128]{2,1,0:T(8,128)S(1)}, u32[]{:S(2)}, u32[]{:S(2)}) collective-permute-start(s32[4,16,128]{2,1,0:T(8,128)S(1)} %pad_add_fusion.1), channel_id=1, source_target_pairs={{0,4},{4,0},{8,12},{12,8},{16,20},{20,16},{24,28},{28,24},{1,5},{5... | collective-permute-start | bytes 98312 | tf_op jit(solution)/shard_map/ppermute | solution.py:346
  38.5 6.5 %collective-permute-start.13 = (bf16[256,256]{1,0:T(8,128)(2,1)S(1)}, bf16[256,256]{1,0:T(8,128)(2,1)S(1)}, u32[]{:S(2)}, u32[]{:S(2)}) collective-permute-start(bf16[256,256]{1,0:T(8,128)(2,1)S(1)} %pad_maximum_fusion.rest_0_), channel_id=1, source_target_pairs={{0,4},{4,0},{8,12},{12,8},{16,20},{20,16},{24,28},{28,24},{1,5},{5... | collective-permute-start | bytes 393224 | tf_op jit(solution)/shard_map/ppermute | solution.py:346
  39.0 7.4 %collective-permute-start.12 = (bf16[256,256]{1,0:T(8,128)(2,1)S(1)}, bf16[256,256]{1,0:T(8,128)(2,1)S(1)}, u32[]{:S(2)}, u32[]{:S(2)}) collective-permute-start(bf16[256,256]{1,0:T(8,128)(2,1)S(1)} %pad_maximum_fusion.rest_0_), channel_id=1, source_target_pairs={{0,24},{4,28},{8,16},{12,20},{16,8},{20,12},{24,0},{28,4},{1,25},{... | collective-permute-start | bytes 393224 | tf_op jit(solution)/shard_map/ppermute | solution.py:346
  41.4 6.7 %collective-permute-start.11 = (bf16[256,256]{1,0:T(8,128)(2,1)S(1)}, bf16[256,256]{1,0:T(8,128)(2,1)S(1)}, u32[]{:S(2)}, u32[]{:S(2)}) collective-permute-start(bf16[256,256]{1,0:T(8,128)(2,1)S(1)} %pad_maximum_fusion.rest_0_), channel_id=1, source_target_pairs={{0,16},{4,20},{8,24},{12,28},{16,0},{20,4},{24,8},{28,12},{1,17},{... | collective-permute-start | bytes 393224 | tf_op jit(solution)/shard_map/ppermute | solution.py:346
  41.9 6.3 %collective-permute-start.10 = (bf16[256,256]{1,0:T(8,128)(2,1)S(1)}, bf16[256,256]{1,0:T(8,128)(2,1)S(1)}, u32[]{:S(2)}, u32[]{:S(2)}) collective-permute-start(bf16[256,256]{1,0:T(8,128)(2,1)S(1)} %pad_maximum_fusion.rest_0_), channel_id=1, source_target_pairs={{0,8},{4,12},{8,0},{12,4},{16,24},{20,28},{24,16},{28,20},{1,9},{5... | collective-permute-start | bytes 393224 | tf_op jit(solution)/shard_map/ppermute | solution.py:346
  45.0 3.7 %copy-start.1 = (s32[32,1]{0,1:T(1,128)S(1)}, s32[32,1]{0,1:T(1,128)}, u32[]{:S(2)}) copy-start(s32[32,1]{0,1:T(1,128)} %param.9) | copy-start | bytes 388
  48.3 1.3 %collective-permute-start.14 = (bf16[256,256]{1,0:T(8,128)(2,1)S(1)}, bf16[256,256]{1,0:T(8,128)(2,1)S(1)}, u32[]{:S(2)}, u32[]{:S(2)}) collective-permute-start(bf16[256,256]{1,0:T(8,128)(2,1)S(1)} %collective-permute-done.10.rest_0_), channel_id=1, source_target_pairs={{0,4},{4,0},{8,12},{12,8},{16,20},{20,16},{24,28},{28,24},{1,5},{5... | collective-permute-start | bytes 393224 | tf_op jit(solution)/shard_map/ppermute | solution.py:346
  48.3 1.5 %collective-permute-start.15 = (bf16[256,256]{1,0:T(8,128)(2,1)S(1)}, bf16[256,256]{1,0:T(8,128)(2,1)S(1)}, u32[]{:S(2)}, u32[]{:S(2)}) collective-permute-start(bf16[256,256]{1,0:T(8,128)(2,1)S(1)} %collective-permute-done.11.rest_2_), channel_id=1, source_target_pairs={{0,4},{4,0},{8,12},{12,8},{16,20},{20,16},{24,28},{28,24},{1,5},{5... | collective-permute-start | bytes 393224 | tf_op jit(solution)/shard_map/ppermute | solution.py:346
  48.8 1.3 %collective-permute-start.16 = (bf16[256,256]{1,0:T(8,128)(2,1)S(1)}, bf16[256,256]{1,0:T(8,128)(2,1)S(1)}, u32[]{:S(2)}, u32[]{:S(2)}) collective-permute-start(bf16[256,256]{1,0:T(8,128)(2,1)S(1)} %collective-permute-done.12.rest_4_), channel_id=1, source_target_pairs={{0,4},{4,0},{8,12},{12,8},{16,20},{20,16},{24,28},{28,24},{1,5},{5... | collective-permute-start | bytes 393224 | tf_op jit(solution)/shard_map/ppermute | solution.py:346

commit v4 on v3

--- a/solution.py
+++ b/solution.py
@@ -210,14 +210,14 @@
     )(targets)
 
 
-def _choose(pick, source_ref, tiles, blocks, rows, period, offset):
+def _choose(pick, source_ref, tiles, starts, rows):
     lane = lax.broadcasted_iota(jnp.int32, (TILE, rows), 1).astype(jnp.bfloat16)
     one = jnp.ones((TILE, rows), jnp.bfloat16)
     zero = jnp.zeros((TILE, rows), jnp.bfloat16)
     for j, t in enumerate(tiles):
         s = jnp.broadcast_to(source_ref[:, t:t + 1], (TILE, rows))
-        for b in range(blocks):
-            here = (s - (b * period + offset)).astype(jnp.bfloat16)
+        for b, start in enumerate(starts):
+            here = (s - start).astype(jnp.bfloat16)
             pick[j * TILE:(j + 1) * TILE, b * rows:(b + 1) * rows] = jnp.where(lane == here, one, zero)
 
 
@@ -227,30 +227,33 @@
         units[b * rows:(b + 1) * rows, :] = ref[...]
 
 
-def _place_kernel(blocks, group, period, offset, source_ref, *rest):
+def _place_kernel(starts, group, has_placed, source_ref, *rest):
+    blocks = len(starts)
     unit_refs = rest[:blocks]
-    table, units, pick = rest[blocks:]
+    placed_ref = rest[blocks] if has_placed else None
+    table, units, pick = rest[blocks + has_placed:]
     rows = unit_refs[0].shape[0]
     _collect(units, unit_refs)
     groups = table.shape[0] // (group * TILE)
     for g in range(-1, groups):
         if g + 1 < groups:
             span = range((g + 1) * group, (g + 2) * group)
-            _choose(pick.at[(g + 1) % 2], source_ref, span, blocks, rows, period, offset)
+            _choose(pick.at[(g + 1) % 2], source_ref, span, starts, rows)
         if g >= 0:
-            table[g * group * TILE:(g + 1) * group * TILE, :] = jnp.dot(
-                pick[g % 2], units[...], preferred_element_type=jnp.float32
-            ).astype(jnp.bfloat16)
-
-
-def _place(source, units, period, offset):
+            span = slice(g * group * TILE, (g + 1) * group * TILE)
+            new = jnp.dot(pick[g % 2], units[...], preferred_element_type=jnp.float32).astype(jnp.bfloat16)
+            table[span, :] = new + placed_ref[span, :] if has_placed else new
+
+
+def _place(source, units, starts, placed):
     tiles = source.shape[1]
     group = _fits(tiles, 4)
     rows, width = units[0].shape
+    extra = [] if placed is None else [placed]
     return pl.pallas_call(
-        functools.partial(_place_kernel, len(units), group, period, offset),
+        functools.partial(_place_kernel, starts, group, len(extra)),
         out_shape=jax.ShapeDtypeStruct((tiles * TILE, width), jnp.bfloat16),
-        in_specs=[pl.BlockSpec(memory_space=pltpu.VMEM)] * (1 + len(units)),
+        in_specs=[pl.BlockSpec(memory_space=pltpu.VMEM)] * (1 + len(units) + len(extra)),
         out_specs=pl.BlockSpec(memory_space=pltpu.VMEM),
         scratch_shapes=[
             pltpu.VMEM((len(units) * rows, width), jnp.bfloat16),
@@ -261,10 +264,11 @@
             flops=2 * tiles * TILE * width * len(units) * rows,
             bytes_accessed=2 * tiles * TILE * width, transcendentals=0,
         ),
-    )(source, *units)
-
-
-def _tiles_kernel(blocks, group, period, offset, has_placed, counts_ref, source_ref, *rest):
+    )(source, *units, *extra)
+
+
+def _tiles_kernel(starts, group, has_placed, counts_ref, source_ref, *rest):
+    blocks = len(starts)
     unit_refs = rest[:blocks]
     placed_ref = rest[blocks] if has_placed else None
     cosine_hbm, affinity_ref, cosine, units, pick, table, sems = rest[blocks + has_placed:]
@@ -301,7 +305,7 @@
     for g in range(-1, groups + 1):
         if g + 1 < groups:
             span = range((g + 1) * group, (g + 2) * group)
-            _choose(pick.at[(g + 1) % 2], source_ref, span, blocks, rows, period, offset)
+            _choose(pick.at[(g + 1) % 2], source_ref, span, starts, rows)
         if 0 <= g < groups:
             place(g)
         if g >= 1:
@@ -310,13 +314,13 @@
         copy_out(g).wait()
 
 
-def _tiles(counts, source, units, placed, period, offset):
+def _tiles(counts, source, units, starts, placed):
     tiles = counts.shape[0]
     group = _fits(tiles, 4)
     rows, width = units[0].shape
     extra = [] if placed is None else [placed]
     return pl.pallas_call(
-        functools.partial(_tiles_kernel, len(units), group, period, offset, len(extra)),
+        functools.partial(_tiles_kernel, starts, group, len(extra)),
         out_shape=[
             jax.ShapeDtypeStruct((tiles, TILE, TILE), jnp.float32),
             jax.ShapeDtypeStruct((tiles, TILE), jnp.float32),
@@ -361,15 +365,27 @@
         lists, first = lax.optimization_barrier((lists, own[0] + received[0]))
         near_lists = jnp.stack(everywhere(targets_of(lists), "docs", n_docs, 2))
         rows_dev = near_lists.shape[1]
-        unit = jnp.concatenate(everywhere(_unit([first] + received[1:]), "feat", n_feat, 1))
+        shards = everywhere(_unit([first] + received[1:]), "feat", n_feat, 1)
+        unit = jnp.zeros((docs, shards[0].shape[1]), jnp.bfloat16)
+        for k in reversed(range(n_feat)):
+            unit = lax.dynamic_update_slice(unit, shards[k], (k * shard, 0))
         unit, near_lists = lax.optimization_barrier((unit, near_lists))
         far = [send(unit, "docs", n_docs, k) for k in range(2, n_docs, 2)]
         targets = jnp.stack([near_lists, send(near_lists, "docs", n_docs, 1)], axis=1).reshape(-1, 128)
         source = _sources(targets, docs, tiles, rows_dev, shard)
-        placed = _place(source, [unit, send(unit, "docs", n_docs, 1)], docs, 0)
-        far, placed = lax.optimization_barrier((far, placed))
-        units = [u for x in far for u in (x, send(x, "docs", n_docs, 1))]
-        cosine, affinity = _tiles(counts, source, units, placed, docs, 2 * docs)
+
+        def swap(x):
+            return send(x, "docs", n_docs, 1)
+
+        at = [docs * k for k in range(n_docs)]
+        placed = _place(source, [unit, swap(unit)], at[:2], None)
+        near, placed = lax.optimization_barrier((far[0], placed))
+        first = swap(near)
+        placed = _place(source, [near], at[2:3], placed)
+        rest, placed = lax.optimization_barrier((far[1:], placed))
+        swapped = [swap(x) for x in rest]
+        placed = _place(source, rest + [first], at[4::2] + at[3:4], placed)
+        cosine, affinity = _tiles(counts, source, swapped, at[5::2], placed)
         return cosine[:, None], affinity[:, None]
 
     placed = (

time: 56.8 us -> 55.5 us (0.977)
  waiting for transfers between devices: 8.1 us -> 6.03 us
  Pallas kernels: 28.4 us -> 29 us
    ppermute x17, waiting for transfers between devices: 8.1 us -> 6.03 us  [send(): return lax.ppermute(x, axis, [(i, i ^ k) for i in range(size)])]
    pallas_call x2 -> x4, Pallas kernels: 7.73 us -> 8.32 us  [the longest x1 4.22 us: _tiles(): pl.pallas_call(functools.partial(_tiles_kernel, starts, group, len(extra)...]
  transfers between devices with their start and end apart: 17 -> 17, of which waited for: 9 -> 5; matrix products, arithmetic and copies ran while one was open for 2% -> 2% of each run, Pallas kernels for 7% -> 12%
where the time goes in v4:
time: 55.5 us; the launch traced here: 55.3 us
  Pallas kernels  29 us (52%)
  starting transfers between devices  18.3 us (33%)
  waiting for transfers between devices  6.03 us (11%)
  between operations  0.95 us (2%)
  other arithmetic  0.86 us (2%)
    ppermute x17, starting transfers between devices, send(): return lax.ppermute(x, axis, [(i, i ^ k) for i in range(size)])  18.3 us
    pallas_call x1, Pallas kernels, _signature_parts(): pl.pallas_call(functools.partial(_signature_kernel, first, docs, entries,...  18.1 us
    ppermute x17, waiting for transfers between devices, send(): return lax.ppermute(x, axis, [(i, i ^ k) for i in range(size)])  6.03 us
    pallas_call x1, Pallas kernels, _tiles(): pl.pallas_call(functools.partial(_tiles_kernel, starts, group, len(extra)...  4.22 us
    pallas_call x3, Pallas kernels, _place(): pl.pallas_call(functools.partial(_place_kernel, starts, group, len(extra)...  4.09 us
    pallas_call x1, Pallas kernels, _sources(): pl.pallas_call(functools.partial(_source_kernel, docs, tiles, rows_dev, s...  2.53 us
  transfers between devices with their start and end apart: 17, of which 5 were waited for; matrix products, arithmetic and copies ran while one was open for 2% of the time, Pallas kernels for 12%

profile of v4, /device:TPU:0, one launch (start us, length us, event | category | flops | bytes accessed | tf_op | source)
XLA Modules:
  0.0 55.3 jit_solution(15143907798913355028)
XLA Ops:
  0.6 18.1 %shard_map.68 = (f32[64,256]{1,0:T(8,128)}, f32[64,256]{1,0:T(8,128)}, f32[64,256]{1,0:T(8,128)}, f32[64,256]{1,0:T(8,128)}) custom-call(s32[256,128]{1,0:T(8,128)} %ids_ref.1, bf16[256,128]{1,0:T(8,128)(2,1)} %w_ref.1, bf16[32768,256]{1,0:T(8,128)(2,1)} %proj_ref.1), custom_call_target="tpu_custom_call" | custom-call | flops 12884901888 | bytes 16777216 | tf_op jit(solution)/shard_map/pallas_call | solution.py:113
  18.7 3.1 %collective-permute-start = (f32[64,256]{1,0:T(8,128)}, f32[64,256]{1,0:T(8,128)S(1)}, u32[]{:S(2)}, u32[]{:S(2)}) collective-permute-start(f32[64,256]{1,0:T(8,128)} %get-tuple-element.18), channel_id=1, source_target_pairs={{0,1},{1,0},{2,3},{3,2},{4,5},{5,4},{6,7},{7,6},{8,9},{9,8},{10,11... | collective-permute-start | bytes 196616 | tf_op jit(solution)/shard_map/ppermute | solution.py:350
  21.8 2.6 %collective-permute-start.1 = (f32[64,256]{1,0:T(8,128)}, f32[64,256]{1,0:T(8,128)S(1)}, u32[]{:S(2)}, u32[]{:S(2)}) collective-permute-start(f32[64,256]{1,0:T(8,128)} %get-tuple-element.20), channel_id=1, source_target_pairs={{0,2},{1,3},{2,0},{3,1},{4,6},{5,7},{6,4},{7,5},{8,10},{9,11},{10,... | collective-permute-start | bytes 196616 | tf_op jit(solution)/shard_map/ppermute | solution.py:350
  24.4 0.0 collective-permute-done
  24.4 0.9 %add.11.refs_0_ = f32[64,256]{1,0:T(8,128)S(1)} add(f32[64,256]{1,0:T(8,128)} %get-tuple-element.17, f32[64,256]{1,0:T(8,128)S(1)} %collective-permute-done) | non-fusion elementwise | flops 16384 | bytes 196608 | tf_op jit(solution)/shard_map/add | solution.py:365
  25.3 1.9 %collective-permute-start.6 = (s32[16,128]{1,0:T(8,128)S(1)}, s32[16,128]{1,0:T(8,128)S(1)}, u32[]{:S(2)}, u32[]{:S(2)}) collective-permute-start(s32[16,128]{1,0:T(8,128)S(1)} %reshape.13), channel_id=1, source_target_pairs={{0,8},{4,12},{8,0},{12,4},{16,24},{20,28},{24,16},{28,20},{1,9},{5... | collective-permute-start | bytes 24584 | tf_op jit(solution)/shard_map/ppermute | solution.py:350
  27.2 1.5 %collective-permute-start.7 = (s32[16,128]{1,0:T(8,128)S(1)}, s32[16,128]{1,0:T(8,128)S(1)}, u32[]{:S(2)}, u32[]{:S(2)}) collective-permute-start(s32[16,128]{1,0:T(8,128)S(1)} %reshape.13), channel_id=1, source_target_pairs={{0,16},{4,20},{8,24},{12,28},{16,0},{20,4},{24,8},{28,12},{1,17},{... | collective-permute-start | bytes 24584 | tf_op jit(solution)/shard_map/ppermute | solution.py:350
  28.7 0.2 collective-permute-start.8
  28.9 0.4 collective-permute-done.1.refs_1_
  29.3 1.4 %collective-permute-done.2.refs_2_ = f32[64,256]{1,0:T(8,128)S(1)} collective-permute-done((f32[64,256]{1,0:T(8,128)}, f32[64,256]{1,0:T(8,128)S(1)}, u32[]{:S(2)}, u32[]{:S(2)}) %collective-permute-start.2) | collective-permute-done | bytes 65568 | tf_op jit(solution)/shard_map/ppermute | solution.py:350
  30.7 0.1 shard_map.69
  30.8 2.8 %collective-permute-start.3 = (bf16[64,256]{1,0:T(8,128)(2,1)S(1)}, bf16[64,256]{1,0:T(8,128)(2,1)S(1)}, u32[]{:S(2)}, u32[]{:S(2)}) collective-permute-start(bf16[64,256]{1,0:T(8,128)(2,1)S(1)} %shard_map.69), channel_id=1, source_target_pairs={{0,3},{1,2},{2,1},{3,0},{4,7},{5,6},{6,5},{7,4},{8,11},{9,10},{10,... | collective-permute-start | bytes 98312 | tf_op jit(solution)/shard_map/ppermute | solution.py:350
  33.6 0.0 collective-permute-start.4
  33.6 1.7 %collective-permute-start.5 = (bf16[64,256]{1,0:T(8,128)(2,1)S(1)}, bf16[64,256]{1,0:T(8,128)(2,1)S(1)}, u32[]{:S(2)}, u32[]{:S(2)}) collective-permute-start(bf16[64,256]{1,0:T(8,128)(2,1)S(1)} %shard_map.69), channel_id=1, source_target_pairs={{0,1},{1,0},{2,3},{3,2},{4,5},{5,4},{6,7},{7,6},{8,9},{9,8},{10,11... | collective-permute-start | bytes 98312 | tf_op jit(solution)/shard_map/ppermute | solution.py:350
  35.2 0.0 collective-permute-done.7
  35.3 1.3 %collective-permute-done.3 = bf16[64,256]{1,0:T(8,128)(2,1)S(1)} collective-permute-done((bf16[64,256]{1,0:T(8,128)(2,1)S(1)}, bf16[64,256]{1,0:T(8,128)(2,1)S(1)}, u32[]{:S(2)}, u32[]{:S(2)}) %collective-permute-start.3) | collective-permute-done | bytes 32800 | tf_op jit(solution)/shard_map/ppermute | solution.py:350
  36.6 1.8 %collective-permute-done.4 = bf16[64,256]{1,0:T(8,128)(2,1)S(1)} collective-permute-done((bf16[64,256]{1,0:T(8,128)(2,1)S(1)}, bf16[64,256]{1,0:T(8,128)(2,1)S(1)}, u32[]{:S(2)}, u32[]{:S(2)}) %collective-permute-start.4) | collective-permute-done | bytes 32800 | tf_op jit(solution)/shard_map/ppermute | solution.py:350
  38.4 0.0 collective-permute-done.5
  38.4 0.1 collective-permute-start.9
  38.5 0.5 collective-permute-start.13
  39.0 1.5 %collective-permute-start.12 = (bf16[256,256]{1,0:T(8,128)(2,1)S(1)}, bf16[256,256]{1,0:T(8,128)(2,1)S(1)}, u32[]{:S(2)}, u32[]{:S(2)}) collective-permute-start(bf16[256,256]{1,0:T(8,128)(2,1)S(1)} %constant_dynamic-update-slice_fusion.rest_0_), channel_id=1, source_target_pairs={{0,8},{4,12},{8,0},{12,4},{16,24},{20,28},{24,16},{28,20},{1,9},{5... | collective-permute-start | bytes 393224 | tf_op jit(solution)/shard_map/ppermute | solution.py:350
  40.5 1.5 %collective-permute-start.10 = (bf16[256,256]{1,0:T(8,128)(2,1)S(1)}, bf16[256,256]{1,0:T(8,128)(2,1)S(1)}, u32[]{:S(2)}, u32[]{:S(2)}) collective-permute-start(bf16[256,256]{1,0:T(8,128)(2,1)S(1)} %constant_dynamic-update-slice_fusion.rest_0_), channel_id=1, source_target_pairs={{0,16},{4,20},{8,24},{12,28},{16,0},{20,4},{24,8},{28,12},{1,17},{... | collective-permute-start | bytes 393224 | tf_op jit(solution)/shard_map/ppermute | solution.py:350
  42.0 0.5 collective-permute-start.11
  42.5 2.5 %shard_map.70.source_ref = f32[128,32]{1,0:T(8,128)S(1)} custom-call(s32[128,128]{1,0:T(8,128)S(1)} %bitcast.18), custom_call_target="tpu_custom_call" | custom-call | flops 536870912 | bytes 65536 | tf_op jit(solution)/shard_map/pallas_call | solution.py:196
  45.0 1.3 %shard_map.71.rest_1_ = bf16[4096,256]{1,0:T(8,128)(2,1)S(1)} custom-call(f32[128,32]{1,0:T(8,128)S(1)} %shard_map.70.source_ref, bf16[256,256]{1,0:T(8,128)(2,1)S(1)} %constant_dynamic-update-slice_fusion.rest_0_, bf16[256,256]{1,0:T(8,128)(2,1)S(1)} %collective-permute-done.13.rest_1_), custom_call_target="tpu_custom_call" | custom-call | flops 1073741824 | bytes 2097152 | tf_op jit(solution)/shard_map/pallas_call | solution.py:253
  46.4 0.1 collective-permute-start.16
  46.5 0.1 copy.14.counts_ref
  46.6 0.9 %shard_map.72.rest_3_ = bf16[4096,256]{1,0:T(8,128)(2,1)S(1)} custom-call(f32[128,32]{1,0:T(8,128)S(1)} %shard_map.70.source_ref, bf16[256,256]{1,0:T(8,128)(2,1)S(1)} %collective-permute-done.12.rest_0_, bf16[4096,256]{1,0:T(8,128)(2,1)S(1)} %shard_map.71.rest_1_), custom_call_target="tpu_custom_call" | custom-call | flops 536870912 | bytes 2097152 | tf_op jit(solution)/shard_map/pallas_call | solution.py:253
  47.4 1.1 %collective-permute-done.10.rest_0_ = bf16[256,256]{1,0:T(8,128)(2,1)S(1)} collective-permute-done((bf16[256,256]{1,0:T(8,128)(2,1)S(1)}, bf16[256,256]{1,0:T(8,128)(2,1)S(1)}, u32[]{:S(2)}, u32[]{:S(2)}) %collective-permute-start.10) | collective-permute-done | bytes 131104 | tf_op jit(solution)/shard_map/ppermute | solution.py:350
  48.5 0.5 collective-permute-start.15
  49.0 1.9 %shard_map.73.rest_2_ = bf16[4096,256]{1,0:T(8,128)(2,1)S(1)} custom-call(f32[128,32]{1,0:T(8,128)S(1)} %shard_map.70.source_ref, bf16[256,256]{1,0:T(8,128)(2,1)S(1)} %collective-permute-done.10.rest_0_, bf16[256,256]{1,0:T(8,128)(2,1)S(1)} %collective-permute-done.11.rest_1_, bf16[256,256]{1,0:T(8,128)(2,1)S(1)} %collective-permute-done.16.rest_2_, ...), custom_call_target="tpu_custom_call" | custom-call | flops 1610612736 | bytes 2097152 | tf_op jit(solution)/shard_map/pallas_call | solution.py:253
  50.9 4.2 %shard_map.74 = (f32[32,128,128]{2,1,0:T(8,128)}, f32[32,128]{1,0:T(8,128)}) custom-call(s32[32,1]{1,0:T(8,128)S(1)} %copy.14.counts_ref, f32[128,32]{1,0:T(8,128)S(1)} %shard_map.70.source_ref, bf16[256,256]{1,0:T(8,128)(2,1)S(1)} %collective-permute-done.14.rest_0_, bf16[256,256]{1,0:T(8,128)(2,1)S(1)} %collective-permute-done.15.rest_1_, ...), custom_call_target="tpu_custom_call" | custom-call | flops 1342177280 | bytes 2097152 | tf_op jit(solution)/shard_map/pallas_call | solution.py:322
  (25 shorter events, 0.1 us)
Async XLA Ops:
  0.6 24.6 %copy-start = (s32[256,8,2]{0,2,1:T(2,128)S(1)}, s32[256,8,2]{0,2,1:T(2,128)}, u32[]{:S(2)}) copy-start(s32[256,8,2]{0,2,1:T(2,128)} %param.8) | copy-start | bytes 49156
  18.7 5.7 %collective-permute-start = (f32[64,256]{1,0:T(8,128)}, f32[64,256]{1,0:T(8,128)S(1)}, u32[]{:S(2)}, u32[]{:S(2)}) collective-permute-start(f32[64,256]{1,0:T(8,128)} %get-tuple-element.18), channel_id=1, source_target_pairs={{0,1},{1,0},{2,3},{3,2},{4,5},{5,4},{6,7},{7,6},{8,9},{9,8},{10,11... | collective-permute-start | bytes 196616 | tf_op jit(solution)/shard_map/ppermute | solution.py:350
  21.8 7.5 %collective-permute-start.1 = (f32[64,256]{1,0:T(8,128)}, f32[64,256]{1,0:T(8,128)S(1)}, u32[]{:S(2)}, u32[]{:S(2)}) collective-permute-start(f32[64,256]{1,0:T(8,128)} %get-tuple-element.20), channel_id=1, source_target_pairs={{0,2},{1,3},{2,0},{3,1},{4,6},{5,7},{6,4},{7,5},{8,10},{9,11},{10,... | collective-permute-start | bytes 196616 | tf_op jit(solution)/shard_map/ppermute | solution.py:350
  24.4 6.3 %collective-permute-start.2 = (f32[64,256]{1,0:T(8,128)}, f32[64,256]{1,0:T(8,128)S(1)}, u32[]{:S(2)}, u32[]{:S(2)}) collective-permute-start(f32[64,256]{1,0:T(8,128)} %get-tuple-element.21), channel_id=1, source_target_pairs={{0,3},{1,2},{2,1},{3,0},{4,7},{5,6},{6,5},{7,4},{8,11},{9,10},{10,... | collective-permute-start | bytes 196616 | tf_op jit(solution)/shard_map/ppermute | solution.py:350
  25.3 8.3 %collective-permute-start.6 = (s32[16,128]{1,0:T(8,128)S(1)}, s32[16,128]{1,0:T(8,128)S(1)}, u32[]{:S(2)}, u32[]{:S(2)}) collective-permute-start(s32[16,128]{1,0:T(8,128)S(1)} %reshape.13), channel_id=1, source_target_pairs={{0,8},{4,12},{8,0},{12,4},{16,24},{20,28},{24,16},{28,20},{1,9},{5... | collective-permute-start | bytes 24584 | tf_op jit(solution)/shard_map/ppermute | solution.py:350
  27.2 8.1 %collective-permute-start.7 = (s32[16,128]{1,0:T(8,128)S(1)}, s32[16,128]{1,0:T(8,128)S(1)}, u32[]{:S(2)}, u32[]{:S(2)}) collective-permute-start(s32[16,128]{1,0:T(8,128)S(1)} %reshape.13), channel_id=1, source_target_pairs={{0,16},{4,20},{8,24},{12,28},{16,0},{20,4},{24,8},{28,12},{1,17},{... | collective-permute-start | bytes 24584 | tf_op jit(solution)/shard_map/ppermute | solution.py:350
  28.7 6.6 %collective-permute-start.8 = (s32[16,128]{1,0:T(8,128)S(1)}, s32[16,128]{1,0:T(8,128)S(1)}, u32[]{:S(2)}, u32[]{:S(2)}) collective-permute-start(s32[16,128]{1,0:T(8,128)S(1)} %reshape.13), channel_id=1, source_target_pairs={{0,24},{4,28},{8,16},{12,20},{16,8},{20,12},{24,0},{28,4},{1,25},{... | collective-permute-start | bytes 24584 | tf_op jit(solution)/shard_map/ppermute | solution.py:350
  30.8 5.8 %collective-permute-start.3 = (bf16[64,256]{1,0:T(8,128)(2,1)S(1)}, bf16[64,256]{1,0:T(8,128)(2,1)S(1)}, u32[]{:S(2)}, u32[]{:S(2)}) collective-permute-start(bf16[64,256]{1,0:T(8,128)(2,1)S(1)} %shard_map.69), channel_id=1, source_target_pairs={{0,3},{1,2},{2,1},{3,0},{4,7},{5,6},{6,5},{7,4},{8,11},{9,10},{10,... | collective-permute-start | bytes 98312 | tf_op jit(solution)/shard_map/ppermute | solution.py:350
  33.6 4.8 %collective-permute-start.4 = (bf16[64,256]{1,0:T(8,128)(2,1)S(1)}, bf16[64,256]{1,0:T(8,128)(2,1)S(1)}, u32[]{:S(2)}, u32[]{:S(2)}) collective-permute-start(bf16[64,256]{1,0:T(8,128)(2,1)S(1)} %shard_map.69), channel_id=1, source_target_pairs={{0,2},{1,3},{2,0},{3,1},{4,6},{5,7},{6,4},{7,5},{8,10},{9,11},{10,... | collective-permute-start | bytes 98312 | tf_op jit(solution)/shard_map/ppermute | solution.py:350
  33.6 4.8 %collective-permute-start.5 = (bf16[64,256]{1,0:T(8,128)(2,1)S(1)}, bf16[64,256]{1,0:T(8,128)(2,1)S(1)}, u32[]{:S(2)}, u32[]{:S(2)}) collective-permute-start(bf16[64,256]{1,0:T(8,128)(2,1)S(1)} %shard_map.69), channel_id=1, source_target_pairs={{0,1},{1,0},{2,3},{3,2},{4,5},{5,4},{6,7},{7,6},{8,9},{9,8},{10,11... | collective-permute-start | bytes 98312 | tf_op jit(solution)/shard_map/ppermute | solution.py:350
  38.4 4.1 %collective-permute-start.9 = (s32[4,16,128]{2,1,0:T(8,128)S(1)}, s32[4,16,128]{2,1,0:T(8,128)S(1)}, u32[]{:S(2)}, u32[]{:S(2)}) collective-permute-start(s32[4,16,128]{2,1,0:T(8,128)S(1)} %pad_add_fusion.1), channel_id=1, source_target_pairs={{0,4},{4,0},{8,12},{12,8},{16,20},{20,16},{24,28},{28,24},{1,5},{5... | collective-permute-start | bytes 98312 | tf_op jit(solution)/shard_map/ppermute | solution.py:350
  38.5 6.5 %collective-permute-start.13 = (bf16[256,256]{1,0:T(8,128)(2,1)S(1)}, bf16[256,256]{1,0:T(8,128)(2,1)S(1)}, u32[]{:S(2)}, u32[]{:S(2)}) collective-permute-start(bf16[256,256]{1,0:T(8,128)(2,1)S(1)} %constant_dynamic-update-slice_fusion.rest_0_), channel_id=1, source_target_pairs={{0,4},{4,0},{8,12},{12,8},{16,20},{20,16},{24,28},{28,24},{1,5},{5... | collective-permute-start | bytes 393224 | tf_op jit(solution)/shard_map/ppermute | solution.py:350
  39.0 7.4 %collective-permute-start.12 = (bf16[256,256]{1,0:T(8,128)(2,1)S(1)}, bf16[256,256]{1,0:T(8,128)(2,1)S(1)}, u32[]{:S(2)}, u32[]{:S(2)}) collective-permute-start(bf16[256,256]{1,0:T(8,128)(2,1)S(1)} %constant_dynamic-update-slice_fusion.rest_0_), channel_id=1, source_target_pairs={{0,8},{4,12},{8,0},{12,4},{16,24},{20,28},{24,16},{28,20},{1,9},{5... | collective-permute-start | bytes 393224 | tf_op jit(solution)/shard_map/ppermute | solution.py:350
  40.5 8.0 %collective-permute-start.10 = (bf16[256,256]{1,0:T(8,128)(2,1)S(1)}, bf16[256,256]{1,0:T(8,128)(2,1)S(1)}, u32[]{:S(2)}, u32[]{:S(2)}) collective-permute-start(bf16[256,256]{1,0:T(8,128)(2,1)S(1)} %constant_dynamic-update-slice_fusion.rest_0_), channel_id=1, source_target_pairs={{0,16},{4,20},{8,24},{12,28},{16,0},{20,4},{24,8},{28,12},{1,17},{... | collective-permute-start | bytes 393224 | tf_op jit(solution)/shard_map/ppermute | solution.py:350
  42.0 6.5 %collective-permute-start.11 = (bf16[256,256]{1,0:T(8,128)(2,1)S(1)}, bf16[256,256]{1,0:T(8,128)(2,1)S(1)}, u32[]{:S(2)}, u32[]{:S(2)}) collective-permute-start(bf16[256,256]{1,0:T(8,128)(2,1)S(1)} %constant_dynamic-update-slice_fusion.rest_0_), channel_id=1, source_target_pairs={{0,24},{4,28},{8,16},{12,20},{16,8},{20,12},{24,0},{28,4},{1,25},{... | collective-permute-start | bytes 393224 | tf_op jit(solution)/shard_map/ppermute | solution.py:350
  45.0 1.5 %copy-start.1 = (s32[32,1]{0,1:T(1,128)S(1)}, s32[32,1]{0,1:T(1,128)}, u32[]{:S(2)}) copy-start(s32[32,1]{0,1:T(1,128)} %param.9) | copy-start | bytes 388
  46.4 2.6 %collective-permute-start.16 = (bf16[256,256]{1,0:T(8,128)(2,1)S(1)}, bf16[256,256]{1,0:T(8,128)(2,1)S(1)}, u32[]{:S(2)}, u32[]{:S(2)}) collective-permute-start(bf16[256,256]{1,0:T(8,128)(2,1)S(1)} %collective-permute-done.12.rest_0_), channel_id=1, source_target_pairs={{0,4},{4,0},{8,12},{12,8},{16,20},{20,16},{24,28},{28,24},{1,5},{5... | collective-permute-start | bytes 393224 | tf_op jit(solution)/shard_map/ppermute | solution.py:350
  48.5 2.4 %collective-permute-start.14 = (bf16[256,256]{1,0:T(8,128)(2,1)S(1)}, bf16[256,256]{1,0:T(8,128)(2,1)S(1)}, u32[]{:S(2)}, u32[]{:S(2)}) collective-permute-start(bf16[256,256]{1,0:T(8,128)(2,1)S(1)} %collective-permute-done.10.rest_0_), channel_id=1, source_target_pairs={{0,4},{4,0},{8,12},{12,8},{16,20},{20,16},{24,28},{28,24},{1,5},{5... | collective-permute-start | bytes 393224 | tf_op jit(solution)/shard_map/ppermute | solution.py:350
  48.5 2.4 %collective-permute-start.15 = (bf16[256,256]{1,0:T(8,128)(2,1)S(1)}, bf16[256,256]{1,0:T(8,128)(2,1)S(1)}, u32[]{:S(2)}, u32[]{:S(2)}) collective-permute-start(bf16[256,256]{1,0:T(8,128)(2,1)S(1)} %collective-permute-done.11.rest_1_), channel_id=1, source_target_pairs={{0,4},{4,0},{8,12},{12,8},{16,20},{20,16},{24,28},{28,24},{1,5},{5... | collective-permute-start | bytes 393224 | tf_op jit(solution)/shard_map/ppermute | solution.py:350

commit v5 on v4

--- a/solution.py
+++ b/solution.py
@@ -379,13 +379,13 @@
 
         at = [docs * k for k in range(n_docs)]
         placed = _place(source, [unit, swap(unit)], at[:2], None)
-        near, placed = lax.optimization_barrier((far[0], placed))
+        near, placed = lax.optimization_barrier((far[-1], placed))
         first = swap(near)
-        placed = _place(source, [near], at[2:3], placed)
-        rest, placed = lax.optimization_barrier((far[1:], placed))
+        placed = _place(source, [near], at[-2:-1], placed)
+        rest, placed = lax.optimization_barrier((far[:-1], placed))
         swapped = [swap(x) for x in rest]
-        placed = _place(source, rest + [first], at[4::2] + at[3:4], placed)
-        cosine, affinity = _tiles(counts, source, swapped, at[5::2], placed)
+        placed = _place(source, rest + [first], at[2:-2:2] + at[-1:], placed)
+        cosine, affinity = _tiles(counts, source, swapped, at[3:-1:2], placed)
         return cosine[:, None], affinity[:, None]
 
     placed = (

time: 55.5 us -> 55.2 us (level)
  no operation moved by 1% of the time
where the time goes in v5:
time: 55.2 us; the launch traced here: 55.1 us
  Pallas kernels  29 us (53%)
  starting transfers between devices  18.3 us (33%)
  waiting for transfers between devices  5.77 us (10%)
  between operations  0.95 us (2%)
  other arithmetic  0.86 us (2%)
    ppermute x17, starting transfers between devices, send(): return lax.ppermute(x, axis, [(i, i ^ k) for i in range(size)])  18.3 us
    pallas_call x1, Pallas kernels, _signature_parts(): pl.pallas_call(functools.partial(_signature_kernel, first, docs, entries,...  18.1 us
    ppermute x17, waiting for transfers between devices, send(): return lax.ppermute(x, axis, [(i, i ^ k) for i in range(size)])  5.77 us
    pallas_call x1, Pallas kernels, _tiles(): pl.pallas_call(functools.partial(_tiles_kernel, starts, group, len(extra)...  4.23 us
    pallas_call x3, Pallas kernels, _place(): pl.pallas_call(functools.partial(_place_kernel, starts, group, len(extra)...  4.1 us
    pallas_call x1, Pallas kernels, _sources(): pl.pallas_call(functools.partial(_source_kernel, docs, tiles, rows_dev, s...  2.53 us
  transfers between devices with their start and end apart: 17, of which 5 were waited for; matrix products, arithmetic and copies ran while one was open for 2% of the time, Pallas kernels for 12%

profile of v5, /device:TPU:0, one launch (start us, length us, event | category | flops | bytes accessed | tf_op | source)
XLA Modules:
  0.0 55.1 jit_solution(5871669886580574349)
XLA Ops:
  0.6 18.1 %shard_map.68 = (f32[64,256]{1,0:T(8,128)}, f32[64,256]{1,0:T(8,128)}, f32[64,256]{1,0:T(8,128)}, f32[64,256]{1,0:T(8,128)}) custom-call(s32[256,128]{1,0:T(8,128)} %ids_ref.1, bf16[256,128]{1,0:T(8,128)(2,1)} %w_ref.1, bf16[32768,256]{1,0:T(8,128)(2,1)} %proj_ref.1), custom_call_target="tpu_custom_call" | custom-call | flops 12884901888 | bytes 16777216 | tf_op jit(solution)/shard_map/pallas_call | solution.py:113
  18.7 3.1 %collective-permute-start = (f32[64,256]{1,0:T(8,128)}, f32[64,256]{1,0:T(8,128)S(1)}, u32[]{:S(2)}, u32[]{:S(2)}) collective-permute-start(f32[64,256]{1,0:T(8,128)} %get-tuple-element.18), channel_id=1, source_target_pairs={{0,1},{1,0},{2,3},{3,2},{4,5},{5,4},{6,7},{7,6},{8,9},{9,8},{10,11... | collective-permute-start | bytes 196616 | tf_op jit(solution)/shard_map/ppermute | solution.py:350
  21.8 2.6 %collective-permute-start.1 = (f32[64,256]{1,0:T(8,128)}, f32[64,256]{1,0:T(8,128)S(1)}, u32[]{:S(2)}, u32[]{:S(2)}) collective-permute-start(f32[64,256]{1,0:T(8,128)} %get-tuple-element.20), channel_id=1, source_target_pairs={{0,2},{1,3},{2,0},{3,1},{4,6},{5,7},{6,4},{7,5},{8,10},{9,11},{10,... | collective-permute-start | bytes 196616 | tf_op jit(solution)/shard_map/ppermute | solution.py:350
  24.4 0.0 collective-permute-start.2
  24.4 0.9 %add.11.refs_0_ = f32[64,256]{1,0:T(8,128)S(1)} add(f32[64,256]{1,0:T(8,128)} %get-tuple-element.17, f32[64,256]{1,0:T(8,128)S(1)} %collective-permute-done) | non-fusion elementwise | flops 16384 | bytes 196608 | tf_op jit(solution)/shard_map/add | solution.py:365
  25.3 1.9 %collective-permute-start.6 = (s32[16,128]{1,0:T(8,128)S(1)}, s32[16,128]{1,0:T(8,128)S(1)}, u32[]{:S(2)}, u32[]{:S(2)}) collective-permute-start(s32[16,128]{1,0:T(8,128)S(1)} %reshape.13), channel_id=1, source_target_pairs={{0,8},{4,12},{8,0},{12,4},{16,24},{20,28},{24,16},{28,20},{1,9},{5... | collective-permute-start | bytes 24584 | tf_op jit(solution)/shard_map/ppermute | solution.py:350
  27.2 1.5 %collective-permute-start.7 = (s32[16,128]{1,0:T(8,128)S(1)}, s32[16,128]{1,0:T(8,128)S(1)}, u32[]{:S(2)}, u32[]{:S(2)}) collective-permute-start(s32[16,128]{1,0:T(8,128)S(1)} %reshape.13), channel_id=1, source_target_pairs={{0,16},{4,20},{8,24},{12,28},{16,0},{20,4},{24,8},{28,12},{1,17},{... | collective-permute-start | bytes 24584 | tf_op jit(solution)/shard_map/ppermute | solution.py:350
  28.7 0.2 collective-permute-start.8
  28.9 0.4 collective-permute-done.1.refs_1_
  29.3 1.4 %collective-permute-done.2.refs_2_ = f32[64,256]{1,0:T(8,128)S(1)} collective-permute-done((f32[64,256]{1,0:T(8,128)}, f32[64,256]{1,0:T(8,128)S(1)}, u32[]{:S(2)}, u32[]{:S(2)}) %collective-permute-start.2) | collective-permute-done | bytes 65568 | tf_op jit(solution)/shard_map/ppermute | solution.py:350
  30.7 0.1 shard_map.69
  30.8 2.8 %collective-permute-start.3 = (bf16[64,256]{1,0:T(8,128)(2,1)S(1)}, bf16[64,256]{1,0:T(8,128)(2,1)S(1)}, u32[]{:S(2)}, u32[]{:S(2)}) collective-permute-start(bf16[64,256]{1,0:T(8,128)(2,1)S(1)} %shard_map.69), channel_id=1, source_target_pairs={{0,3},{1,2},{2,1},{3,0},{4,7},{5,6},{6,5},{7,4},{8,11},{9,10},{10,... | collective-permute-start | bytes 98312 | tf_op jit(solution)/shard_map/ppermute | solution.py:350
  33.6 0.0 collective-permute-done.6
  33.6 1.7 %collective-permute-start.5 = (bf16[64,256]{1,0:T(8,128)(2,1)S(1)}, bf16[64,256]{1,0:T(8,128)(2,1)S(1)}, u32[]{:S(2)}, u32[]{:S(2)}) collective-permute-start(bf16[64,256]{1,0:T(8,128)(2,1)S(1)} %shard_map.69), channel_id=1, source_target_pairs={{0,1},{1,0},{2,3},{3,2},{4,5},{5,4},{6,7},{7,6},{8,9},{9,8},{10,11... | collective-permute-start | bytes 98312 | tf_op jit(solution)/shard_map/ppermute | solution.py:350
  35.2 0.0 collective-permute-done.7
  35.3 0.0 collective-permute-done.8
  35.3 1.3 %collective-permute-done.3 = bf16[64,256]{1,0:T(8,128)(2,1)S(1)} collective-permute-done((bf16[64,256]{1,0:T(8,128)(2,1)S(1)}, bf16[64,256]{1,0:T(8,128)(2,1)S(1)}, u32[]{:S(2)}, u32[]{:S(2)}) %collective-permute-start.3) | collective-permute-done | bytes 32800 | tf_op jit(solution)/shard_map/ppermute | solution.py:350
  36.6 1.8 %collective-permute-done.4 = bf16[64,256]{1,0:T(8,128)(2,1)S(1)} collective-permute-done((bf16[64,256]{1,0:T(8,128)(2,1)S(1)}, bf16[64,256]{1,0:T(8,128)(2,1)S(1)}, u32[]{:S(2)}, u32[]{:S(2)}) %collective-permute-start.4) | collective-permute-done | bytes 32800 | tf_op jit(solution)/shard_map/ppermute | solution.py:350
  38.4 0.1 collective-permute-start.9
  38.5 0.5 collective-permute-start.13
  39.0 2.4 %collective-permute-start.12 = (bf16[256,256]{1,0:T(8,128)(2,1)S(1)}, bf16[256,256]{1,0:T(8,128)(2,1)S(1)}, u32[]{:S(2)}, u32[]{:S(2)}) collective-permute-start(bf16[256,256]{1,0:T(8,128)(2,1)S(1)} %constant_dynamic-update-slice_fusion.rest_0_), channel_id=1, source_target_pairs={{0,24},{4,28},{8,16},{12,20},{16,8},{20,12},{24,0},{28,4},{1,25},{... | collective-permute-start | bytes 393224 | tf_op jit(solution)/shard_map/ppermute | solution.py:350
  41.4 0.5 collective-permute-start.10
  42.0 0.5 collective-permute-start.11
  42.5 2.5 %shard_map.70.source_ref = f32[128,32]{1,0:T(8,128)S(1)} custom-call(s32[128,128]{1,0:T(8,128)S(1)} %bitcast.18), custom_call_target="tpu_custom_call" | custom-call | flops 536870912 | bytes 65536 | tf_op jit(solution)/shard_map/pallas_call | solution.py:196
  45.0 1.3 %shard_map.71.rest_1_ = bf16[4096,256]{1,0:T(8,128)(2,1)S(1)} custom-call(f32[128,32]{1,0:T(8,128)S(1)} %shard_map.70.source_ref, bf16[256,256]{1,0:T(8,128)(2,1)S(1)} %constant_dynamic-update-slice_fusion.rest_0_, bf16[256,256]{1,0:T(8,128)(2,1)S(1)} %collective-permute-done.13.rest_1_), custom_call_target="tpu_custom_call" | custom-call | flops 1073741824 | bytes 2097152 | tf_op jit(solution)/shard_map/pallas_call | solution.py:253
  46.4 0.1 collective-permute-start.16
  46.5 0.1 copy.14.counts_ref
  46.6 0.9 %shard_map.72.rest_3_ = bf16[4096,256]{1,0:T(8,128)(2,1)S(1)} custom-call(f32[128,32]{1,0:T(8,128)S(1)} %shard_map.70.source_ref, bf16[256,256]{1,0:T(8,128)(2,1)S(1)} %collective-permute-done.12.rest_0_, bf16[4096,256]{1,0:T(8,128)(2,1)S(1)} %shard_map.71.rest_1_), custom_call_target="tpu_custom_call" | custom-call | flops 536870912 | bytes 2097152 | tf_op jit(solution)/shard_map/pallas_call | solution.py:253
  47.4 0.8 %collective-permute-done.10.rest_0_ = bf16[256,256]{1,0:T(8,128)(2,1)S(1)} collective-permute-done((bf16[256,256]{1,0:T(8,128)(2,1)S(1)}, bf16[256,256]{1,0:T(8,128)(2,1)S(1)}, u32[]{:S(2)}, u32[]{:S(2)}) %collective-permute-start.10) | collective-permute-done | bytes 131104 | tf_op jit(solution)/shard_map/ppermute | solution.py:350
  48.2 0.5 collective-permute-start.15
  48.8 1.9 %shard_map.73.rest_2_ = bf16[4096,256]{1,0:T(8,128)(2,1)S(1)} custom-call(f32[128,32]{1,0:T(8,128)S(1)} %shard_map.70.source_ref, bf16[256,256]{1,0:T(8,128)(2,1)S(1)} %collective-permute-done.10.rest_0_, bf16[256,256]{1,0:T(8,128)(2,1)S(1)} %collective-permute-done.11.rest_1_, bf16[256,256]{1,0:T(8,128)(2,1)S(1)} %collective-permute-done.16.rest_2_, ...), custom_call_target="tpu_custom_call" | custom-call | flops 1610612736 | bytes 2097152 | tf_op jit(solution)/shard_map/pallas_call | solution.py:253
  50.7 4.2 %shard_map.74 = (f32[32,128,128]{2,1,0:T(8,128)}, f32[32,128]{1,0:T(8,128)}) custom-call(s32[32,1]{1,0:T(8,128)S(1)} %copy.14.counts_ref, f32[128,32]{1,0:T(8,128)S(1)} %shard_map.70.source_ref, bf16[256,256]{1,0:T(8,128)(2,1)S(1)} %collective-permute-done.14.rest_0_, bf16[256,256]{1,0:T(8,128)(2,1)S(1)} %collective-permute-done.15.rest_1_, ...), custom_call_target="tpu_custom_call" | custom-call | flops 1342177280 | bytes 2097152 | tf_op jit(solution)/shard_map/pallas_call | solution.py:322
  (25 shorter events, 0.1 us)
Async XLA Ops:
  0.6 24.6 %copy-start = (s32[256,8,2]{0,2,1:T(2,128)S(1)}, s32[256,8,2]{0,2,1:T(2,128)}, u32[]{:S(2)}) copy-start(s32[256,8,2]{0,2,1:T(2,128)} %param.8) | copy-start | bytes 49156
  18.7 5.7 %collective-permute-start = (f32[64,256]{1,0:T(8,128)}, f32[64,256]{1,0:T(8,128)S(1)}, u32[]{:S(2)}, u32[]{:S(2)}) collective-permute-start(f32[64,256]{1,0:T(8,128)} %get-tuple-element.18), channel_id=1, source_target_pairs={{0,1},{1,0},{2,3},{3,2},{4,5},{5,4},{6,7},{7,6},{8,9},{9,8},{10,11... | collective-permute-start | bytes 196616 | tf_op jit(solution)/shard_map/ppermute | solution.py:350
  21.8 7.5 %collective-permute-start.1 = (f32[64,256]{1,0:T(8,128)}, f32[64,256]{1,0:T(8,128)S(1)}, u32[]{:S(2)}, u32[]{:S(2)}) collective-permute-start(f32[64,256]{1,0:T(8,128)} %get-tuple-element.20), channel_id=1, source_target_pairs={{0,2},{1,3},{2,0},{3,1},{4,6},{5,7},{6,4},{7,5},{8,10},{9,11},{10,... | collective-permute-start | bytes 196616 | tf_op jit(solution)/shard_map/ppermute | solution.py:350
  24.4 6.3 %collective-permute-start.2 = (f32[64,256]{1,0:T(8,128)}, f32[64,256]{1,0:T(8,128)S(1)}, u32[]{:S(2)}, u32[]{:S(2)}) collective-permute-start(f32[64,256]{1,0:T(8,128)} %get-tuple-element.21), channel_id=1, source_target_pairs={{0,3},{1,2},{2,1},{3,0},{4,7},{5,6},{6,5},{7,4},{8,11},{9,10},{10,... | collective-permute-start | bytes 196616 | tf_op jit(solution)/shard_map/ppermute | solution.py:350
  25.3 8.3 %collective-permute-start.6 = (s32[16,128]{1,0:T(8,128)S(1)}, s32[16,128]{1,0:T(8,128)S(1)}, u32[]{:S(2)}, u32[]{:S(2)}) collective-permute-start(s32[16,128]{1,0:T(8,128)S(1)} %reshape.13), channel_id=1, source_target_pairs={{0,8},{4,12},{8,0},{12,4},{16,24},{20,28},{24,16},{28,20},{1,9},{5... | collective-permute-start | bytes 24584 | tf_op jit(solution)/shard_map/ppermute | solution.py:350
  27.2 8.1 %collective-permute-start.7 = (s32[16,128]{1,0:T(8,128)S(1)}, s32[16,128]{1,0:T(8,128)S(1)}, u32[]{:S(2)}, u32[]{:S(2)}) collective-permute-start(s32[16,128]{1,0:T(8,128)S(1)} %reshape.13), channel_id=1, source_target_pairs={{0,16},{4,20},{8,24},{12,28},{16,0},{20,4},{24,8},{28,12},{1,17},{... | collective-permute-start | bytes 24584 | tf_op jit(solution)/shard_map/ppermute | solution.py:350
  28.7 6.6 %collective-permute-start.8 = (s32[16,128]{1,0:T(8,128)S(1)}, s32[16,128]{1,0:T(8,128)S(1)}, u32[]{:S(2)}, u32[]{:S(2)}) collective-permute-start(s32[16,128]{1,0:T(8,128)S(1)} %reshape.13), channel_id=1, source_target_pairs={{0,24},{4,28},{8,16},{12,20},{16,8},{20,12},{24,0},{28,4},{1,25},{... | collective-permute-start | bytes 24584 | tf_op jit(solution)/shard_map/ppermute | solution.py:350
  30.8 5.8 %collective-permute-start.3 = (bf16[64,256]{1,0:T(8,128)(2,1)S(1)}, bf16[64,256]{1,0:T(8,128)(2,1)S(1)}, u32[]{:S(2)}, u32[]{:S(2)}) collective-permute-start(bf16[64,256]{1,0:T(8,128)(2,1)S(1)} %shard_map.69), channel_id=1, source_target_pairs={{0,3},{1,2},{2,1},{3,0},{4,7},{5,6},{6,5},{7,4},{8,11},{9,10},{10,... | collective-permute-start | bytes 98312 | tf_op jit(solution)/shard_map/ppermute | solution.py:350
  33.6 4.8 %collective-permute-start.4 = (bf16[64,256]{1,0:T(8,128)(2,1)S(1)}, bf16[64,256]{1,0:T(8,128)(2,1)S(1)}, u32[]{:S(2)}, u32[]{:S(2)}) collective-permute-start(bf16[64,256]{1,0:T(8,128)(2,1)S(1)} %shard_map.69), channel_id=1, source_target_pairs={{0,2},{1,3},{2,0},{3,1},{4,6},{5,7},{6,4},{7,5},{8,10},{9,11},{10,... | collective-permute-start | bytes 98312 | tf_op jit(solution)/shard_map/ppermute | solution.py:350
  33.6 4.8 %collective-permute-start.5 = (bf16[64,256]{1,0:T(8,128)(2,1)S(1)}, bf16[64,256]{1,0:T(8,128)(2,1)S(1)}, u32[]{:S(2)}, u32[]{:S(2)}) collective-permute-start(bf16[64,256]{1,0:T(8,128)(2,1)S(1)} %shard_map.69), channel_id=1, source_target_pairs={{0,1},{1,0},{2,3},{3,2},{4,5},{5,4},{6,7},{7,6},{8,9},{9,8},{10,11... | collective-permute-start | bytes 98312 | tf_op jit(solution)/shard_map/ppermute | solution.py:350
  38.4 4.1 %collective-permute-start.9 = (s32[4,16,128]{2,1,0:T(8,128)S(1)}, s32[4,16,128]{2,1,0:T(8,128)S(1)}, u32[]{:S(2)}, u32[]{:S(2)}) collective-permute-start(s32[4,16,128]{2,1,0:T(8,128)S(1)} %pad_add_fusion.1), channel_id=1, source_target_pairs={{0,4},{4,0},{8,12},{12,8},{16,20},{20,16},{24,28},{28,24},{1,5},{5... | collective-permute-start | bytes 98312 | tf_op jit(solution)/shard_map/ppermute | solution.py:350
  38.5 6.5 %collective-permute-start.13 = (bf16[256,256]{1,0:T(8,128)(2,1)S(1)}, bf16[256,256]{1,0:T(8,128)(2,1)S(1)}, u32[]{:S(2)}, u32[]{:S(2)}) collective-permute-start(bf16[256,256]{1,0:T(8,128)(2,1)S(1)} %constant_dynamic-update-slice_fusion.rest_0_), channel_id=1, source_target_pairs={{0,4},{4,0},{8,12},{12,8},{16,20},{20,16},{24,28},{28,24},{1,5},{5... | collective-permute-start | bytes 393224 | tf_op jit(solution)/shard_map/ppermute | solution.py:350
  39.0 7.4 %collective-permute-start.12 = (bf16[256,256]{1,0:T(8,128)(2,1)S(1)}, bf16[256,256]{1,0:T(8,128)(2,1)S(1)}, u32[]{:S(2)}, u32[]{:S(2)}) collective-permute-start(bf16[256,256]{1,0:T(8,128)(2,1)S(1)} %constant_dynamic-update-slice_fusion.rest_0_), channel_id=1, source_target_pairs={{0,24},{4,28},{8,16},{12,20},{16,8},{20,12},{24,0},{28,4},{1,25},{... | collective-permute-start | bytes 393224 | tf_op jit(solution)/shard_map/ppermute | solution.py:350
  41.4 6.8 %collective-permute-start.10 = (bf16[256,256]{1,0:T(8,128)(2,1)S(1)}, bf16[256,256]{1,0:T(8,128)(2,1)S(1)}, u32[]{:S(2)}, u32[]{:S(2)}) collective-permute-start(bf16[256,256]{1,0:T(8,128)(2,1)S(1)} %constant_dynamic-update-slice_fusion.rest_0_), channel_id=1, source_target_pairs={{0,8},{4,12},{8,0},{12,4},{16,24},{20,28},{24,16},{28,20},{1,9},{5... | collective-permute-start | bytes 393224 | tf_op jit(solution)/shard_map/ppermute | solution.py:350
  42.0 6.3 %collective-permute-start.11 = (bf16[256,256]{1,0:T(8,128)(2,1)S(1)}, bf16[256,256]{1,0:T(8,128)(2,1)S(1)}, u32[]{:S(2)}, u32[]{:S(2)}) collective-permute-start(bf16[256,256]{1,0:T(8,128)(2,1)S(1)} %constant_dynamic-update-slice_fusion.rest_0_), channel_id=1, source_target_pairs={{0,16},{4,20},{8,24},{12,28},{16,0},{20,4},{24,8},{28,12},{1,17},{... | collective-permute-start | bytes 393224 | tf_op jit(solution)/shard_map/ppermute | solution.py:350
  45.0 1.5 %copy-start.1 = (s32[32,1]{0,1:T(1,128)S(1)}, s32[32,1]{0,1:T(1,128)}, u32[]{:S(2)}) copy-start(s32[32,1]{0,1:T(1,128)} %param.9) | copy-start | bytes 388
  46.4 2.4 %collective-permute-start.16 = (bf16[256,256]{1,0:T(8,128)(2,1)S(1)}, bf16[256,256]{1,0:T(8,128)(2,1)S(1)}, u32[]{:S(2)}, u32[]{:S(2)}) collective-permute-start(bf16[256,256]{1,0:T(8,128)(2,1)S(1)} %collective-permute-done.12.rest_0_), channel_id=1, source_target_pairs={{0,4},{4,0},{8,12},{12,8},{16,20},{20,16},{24,28},{28,24},{1,5},{5... | collective-permute-start | bytes 393224 | tf_op jit(solution)/shard_map/ppermute | solution.py:350
  48.2 2.4 %collective-permute-start.14 = (bf16[256,256]{1,0:T(8,128)(2,1)S(1)}, bf16[256,256]{1,0:T(8,128)(2,1)S(1)}, u32[]{:S(2)}, u32[]{:S(2)}) collective-permute-start(bf16[256,256]{1,0:T(8,128)(2,1)S(1)} %collective-permute-done.10.rest_0_), channel_id=1, source_target_pairs={{0,4},{4,0},{8,12},{12,8},{16,20},{20,16},{24,28},{28,24},{1,5},{5... | collective-permute-start | bytes 393224 | tf_op jit(solution)/shard_map/ppermute | solution.py:350
  48.2 2.4 %collective-permute-start.15 = (bf16[256,256]{1,0:T(8,128)(2,1)S(1)}, bf16[256,256]{1,0:T(8,128)(2,1)S(1)}, u32[]{:S(2)}, u32[]{:S(2)}) collective-permute-start(bf16[256,256]{1,0:T(8,128)(2,1)S(1)} %collective-permute-done.11.rest_1_), channel_id=1, source_target_pairs={{0,4},{4,0},{8,12},{12,8},{16,20},{20,16},{24,28},{28,24},{1,5},{5... | collective-permute-start | bytes 393224 | tf_op jit(solution)/shard_map/ppermute | solution.py:350
